TPU v7x, 32 devices: a whole 2x2x4 slice. The times are simulated.
32 devices in a mesh: energy: 16 (over z, y, x), slab: 2 (over core).
Axes of the slice: x: 2, y: 2, z: 4, core: 2. Of those that a mesh axis runs over, the one named last changes fastest.
Arguments:
- green_block: bfloat16 [16, 2, 2, 192, 192], P('energy', 'slab'), may hold values from -0.4375 to 0.4375
- coupling: bfloat16 [16, 2, 2, 192, 192], P('energy', 'slab'), may hold values from -0.4375 to 0.4375
- sigma_lesser: bfloat16 [16, 2, 2, 192, 192], P('energy', 'slab'), may hold values from -6 to 6
- screened: bfloat16 [2, 2, 32, 36864], P('slab', None, None, 'energy'), may hold values from -9 to 9
Outputs:
- sigma_next: bfloat16 [16, 2, 2, 192, 192], P('energy', 'slab')
All inputs are finite; a program needn't handle non-finite values.
Results may differ from a plain program's by a relative error of at most 0.0049.
Values may be sent and summed in bfloat16 or wider, within the bound.
A program may use at most 128 MiB of HBM per device.

v0:
```python
import math

import jax
import jax.numpy as jnp
from jax import lax
from jax.sharding import PartitionSpec as P


def from_behind(value, axis, steps):
    count = lax.axis_size(axis)
    first, last = (max(0, -steps), min(count, count - steps))
    return lax.ppermute(value, axis, [(source, source + steps) for source in range(first, last)])


def product(form, first, second):
    return jnp.einsum(form, first, second, preferred_element_type=jnp.float32)


def sandwich(outer, inner):
    outer_real = outer[:, 0]
    outer_imag = outer[:, 1]
    inner_real = inner[:, 0]
    inner_imag = inner[:, 1]
    forward = "eij,ejk->eik"
    adjoint = "eik,ejk->eij"
    half_real = (
        product(forward, outer_real, inner_real) - product(forward, outer_imag, inner_imag)
    ).astype(jnp.bfloat16)
    half_imag = (
        product(forward, outer_real, inner_imag) + product(forward, outer_imag, inner_real)
    ).astype(jnp.bfloat16)
    full_real = product(adjoint, half_real, outer_real) + product(adjoint, half_imag, outer_imag)
    full_imag = product(adjoint, half_imag, outer_real) - product(adjoint, half_real, outer_imag)
    return jnp.stack([full_real, full_imag], axis=1)


def stacked_tables(count):
    length = 2 * count
    rows = jnp.arange(length, dtype=jnp.int32)
    cols = jnp.arange(count, dtype=jnp.int32)
    phases = rows[:, None] * cols[None, :] % length
    angles = phases.astype(jnp.float32) * (2.0 * math.pi / length)
    cosine = jnp.cos(angles)
    sine = jnp.sin(angles)
    from_real = jnp.concatenate([cosine, -sine], axis=0)
    from_imag = jnp.concatenate([sine, cosine], axis=0)
    forward = jnp.stack([from_real, from_imag], axis=-1).reshape(2 * length, 2 * count)
    to_real = jnp.concatenate([cosine.T, -sine.T], axis=1)
    to_imag = jnp.concatenate([sine.T, cosine.T], axis=1)
    backward = jnp.stack([to_real, to_imag], axis=1).reshape(2 * count, 2 * length)
    return (forward, backward)


def shards(green_block, coupling, sigma_lesser, screened):
    high = lax.Precision.HIGHEST
    green_here = green_block[:, 0]
    couple_here = coupling[:, 0]
    sigma_here = sigma_lesser[:, 0]
    energies_here = green_here.shape[0]
    orbitals = green_here.shape[2]
    own_term = sandwich(green_here, sigma_here)
    couple_before = from_behind(couple_here, "slab", 1)
    made_term = sandwich(couple_before, sigma_here)
    far_term = from_behind(made_term, "slab", -1)
    lesser = (own_term + far_term).reshape(energies_here, 2, orbitals * orbitals)
    columns = lax.all_to_all(lesser, "energy", split_axis=2, concat_axis=0, tiled=True)
    total_energies = columns.shape[0]
    width = columns.shape[2]
    length = 2 * total_energies
    forward, backward = stacked_tables(total_energies)
    stacked = columns.reshape(2 * total_energies, width)
    spectrum = jnp.dot(forward, stacked, precision=high)
    spec_real = spectrum[:length]
    spec_imag = spectrum[length:]
    screen_real = screened[0, 0].astype(jnp.float32)
    screen_imag = screened[0, 1].astype(jnp.float32)
    conv_real = spec_real * screen_real - spec_imag * screen_imag
    conv_imag = spec_real * screen_imag + spec_imag * screen_real
    convolved = jnp.concatenate([conv_real, conv_imag], axis=0)
    back = jnp.dot(backward, convolved, precision=high)
    joined = (back.reshape(total_energies, 2, width) / length).astype(jnp.bfloat16)
    returned = lax.all_to_all(joined, "energy", split_axis=0, concat_axis=2, tiled=True)
    return returned.reshape(energies_here, 1, 2, orbitals, orbitals)


def solution(mesh):
    placed = (
        P("energy", "slab", None, None, None),
        P("energy", "slab", None, None, None),
        P("energy", "slab", None, None, None),
        P("slab", None, None, "energy"),
    )
    return jax.shard_map(
        shards,
        mesh=mesh,
        in_specs=placed,
        out_specs=P("energy", "slab", None, None, None),
        check_vma=False,
    )
```

profile of v0, /device:TPU:0, one launch (start us, length us, event | category | flops | bytes accessed | tf_op | source)
XLA Modules:
  0.0 290.5 jit_solution(13062327500261651517)
XLA Ops:
  0.0 2.4 collective-permute-start
  2.4 1.1 fusion.14
  3.5 1.1 fusion.16
  4.6 1.1 fusion.6
  5.7 1.1 fusion.13
  6.8 1.1 fusion.5
  7.9 1.1 fusion.15
  9.1 1.1 fusion.17
  10.1 1.1 fusion.18
  11.2 1.1 fusion.8
  12.3 0.2 fusion.20
  12.5 1.1 fusion.7
  13.6 0.2 fusion.19
  13.8 0.2 fusion.2
  14.0 0.2 fusion.1
  14.2 1.3 collective-permute-start.1
  15.6 1.1 fusion.3
  16.7 1.1 fusion.4
  17.9 9.7 %copy.15 = f32[1,2,192,192]{1,3,2,0:T(8,128)} copy(f32[1,2,192,192]{3,2,1,0:T(8,128)S(1)} %maximum_add_fusion) | data formatting | bytes 589824 | tf_op jit(solution)/shard_map/reshape | solution.py:65
  27.6 0.5 broadcast.37
  28.1 164.6 %reduce = f32[36864,2]{1,0:T(8,128)} reduce(f32[36864,1,2]{2,1,0:T(1,128)} %bitcast.89, f32[]{:T(128)} %broadcast.37), dimensions={1}, to_apply=%bitcast.77.reduce_sub_computation | reduce | bytes 589828
  192.7 15.5 %reshape.143 = f32[16,1,4608]{2,1,0:T(1,128)} reshape(f32[36864,2]{1,0:T(8,128)} %reduce) | data formatting | bytes 589824
  208.3 7.7 %all-to-all-start = ((f32[16,1,4608]{2,1,0:T(1,128)}), f32[16,1,4608]{2,1,0:T(1,128)S(1)}, u32[]{:S(2)}, u32[]{:S(2)}) async-start(f32[16,1,4608]{2,1,0:T(1,128)} %reshape.143), calls=%async_computation | async-start | bytes 589824 | tf_op jit(solution)/shard_map/all_to_all | solution.py:66
  216.3 10.9 %all-to-all-done = f32[16,1,4608]{2,1,0:T(1,128)S(1)} async-done(((f32[16,1,4608]{2,1,0:T(1,128)}), f32[16,1,4608]{2,1,0:T(1,128)S(1)}, u32[]{:S(2)}, u32[]{:S(2)}) %all-to-all-start) | async-done | bytes 294944 | tf_op jit(solution)/shard_map/all_to_all | solution.py:66
  227.2 1.3 reduce.1
  228.6 36.9 %reshape.144 = f32[36864,1,2]{2,1,0:T(1,128)} reshape(f32[16,4608]{1,0:T(8,128)S(1)} %reduce.1) | data formatting | bytes 589824
  265.5 10.7 %copy.12 = f32[1,2,16,2304]{3,1,2,0:T(2,128)S(1)} copy(f32[1,2,16,2304]{1,3,2,0:T(8,128)} %bitcast.90) | data formatting | bytes 589824 | tf_op jit(solution)/shard_map/all_to_all | solution.py:66
  276.2 0.2 reshape.138
  276.4 0.7 fusion.43
  277.2 0.4 fusion
  277.8 11.8 %all_to_all.30 = bf16[16,2,2304]{2,1,0:T(2,128)(2,1)S(1)} all-to-all(bf16[16,2,2304]{2,1,0:T(2,128)(2,1)S(1)} %copy.13), channel_id=1, replica_groups=mesh['energy'=16,'slab'=2] {'energy'}, dimensions={0} | all-to-all | bytes 294912 | tf_op jit(solution)/shard_map/all_to_all | solution.py:82
  289.6 0.9 reshape.139
  (16 shorter events, 0.8 us)
Async XLA Ops:
  0.0 9.1 %collective-permute-start = (bf16[1,2,192,192]{3,2,1,0:T(8,128)(2,1)}, bf16[1,2,192,192]{3,2,1,0:T(8,128)(2,1)S(1)}, u32[]{:S(2)}, u32[]{:S(2)}) collective-permute-start(bf16[1,2,192,192]{3,2,1,0:T(8,128)(2,1)} %bitcast.112), channel_id=1, source_target_pairs={{0,1},{2,3},{4,5},{6,7},{8,9},{10,11},{12,13},{14,15},{16,17},{18,... | collective-permute-start | bytes 442376 | tf_op jit(solution)/shard_map/ppermute | solution.py:12
  14.2 3.6 %collective-permute-start.1 = (f32[1,2,192,192]{3,2,1,0:T(8,128)S(1)}, f32[1,2,192,192]{3,2,1,0:T(8,128)S(1)}, u32[]{:S(2)}, u32[]{:S(2)}) collective-permute-start(f32[1,2,192,192]{3,2,1,0:T(8,128)S(1)} %pad_maximum_fusion), channel_id=1, source_target_pairs={{1,0},{3,2},{5,4},{7,6},{9,8},{11,10},{13,12},{15,14},{17,16},{19,... | collective-permute-start | bytes 884744 | tf_op jit(solution)/shard_map/ppermute | solution.py:12
  208.3 19.0 %all-to-all-start = ((f32[16,1,4608]{2,1,0:T(1,128)}), f32[16,1,4608]{2,1,0:T(1,128)S(1)}, u32[]{:S(2)}, u32[]{:S(2)}) async-start(f32[16,1,4608]{2,1,0:T(1,128)} %reshape.143), calls=%async_computation | async-start | bytes 589824 | tf_op jit(solution)/shard_map/all_to_all | solution.py:66
  228.6 48.5 %copy-start = (bf16[1,2,32,2304]{3,2,1,0:T(8,128)(2,1)S(1)}, bf16[1,2,32,2304]{3,2,1,0:T(8,128)(2,1)}, u32[]{:S(2)}) copy-start(bf16[1,2,32,2304]{3,2,1,0:T(8,128)(2,1)} %param.7) | copy-start | bytes 884740
where the time goes:
time: 292 us; the launch traced here: 291 us
  other arithmetic  167 us (57%)
  local copies, waits for them, and re-layouts  74.6 us (26%)
  matrix products  15 us (5%)
  blocking collectives  11.8 us (4%)
  starting transfers between devices  11.4 us (4%)
  waiting for transfers between devices  11 us (4%)
    unnamed x1, other arithmetic  165 us
    unnamed x5, local copies, waits for them, and re-layouts  53 us
    dot_general x16, matrix products, product(): return jnp.einsum(form, first, second, preferred_element_type=jnp.float32)  13.9 us
    all_to_all x1, blocking collectives, shards(): lax.all_to_all(joined, 'energy', split_axis=0, concat_axis=2, tiled=True)  11.8 us
    all_to_all x1, waiting for transfers between devices, shards(): lax.all_to_all(lesser, 'energy', split_axis=2, concat_axis=0, tiled=True)  10.9 us
    all_to_all x1, local copies, waits for them, and re-layouts, shards(): lax.all_to_all(lesser, 'energy', split_axis=2, concat_axis=0, tiled=True)  10.7 us
    reshape x1, local copies, waits for them, and re-layouts, shards(): (own_term + far_term).reshape(energies_here, 2, orbitals * orbitals)  9.69 us
    all_to_all x1, starting transfers between devices, shards(): lax.all_to_all(lesser, 'energy', split_axis=2, concat_axis=0, tiled=True)  7.71 us
  transfers between devices with their start and end apart: 3, of which 1 were waited for; matrix products, arithmetic and copies ran while one was open for 3% of the time, Pallas kernels for 0%

commit v1 on v0

v1 whole, which is shorter than its diff:
```python
import functools

import jax
import jax.numpy as jnp
import ml_dtypes
import numpy as np
from jax import lax
from jax.experimental import pallas as pl
from jax.experimental.pallas import tpu as pltpu
from jax.sharding import PartitionSpec as P

MESH = pl.DeviceIdType.MESH
LANES = 128
PITCH = 16


def split(table):
    high = table.astype(ml_dtypes.bfloat16)
    low = (table - high.astype(np.float64)).astype(ml_dtypes.bfloat16)
    return high, low


def make_tables(count, rows, pitch):
    length = 2 * count
    phases = np.outer(np.arange(length), np.arange(count)) % length
    angles = phases * (2.0 * np.pi / length)
    forward, backward = [], []
    same = np.zeros((rows, pitch))
    same[np.arange(rows), np.arange(rows)] = 1.0
    for table in (np.cos(angles), np.sin(angles)):
        wide = np.einsum("ke,rs->rkes", table, same).reshape(rows * length, count * pitch)
        forward.append(split(wide))
        backward.append(split(wide.T / length))
    tables = []
    for pair in (forward, backward):
        tables.append(np.concatenate([pair[0][0], pair[1][0], pair[0][1], pair[1][1]], axis=0))
    spread = np.zeros((count * pitch, count * rows), ml_dtypes.bfloat16)
    for owner in range(count):
        for row in range(rows):
            spread[owner * pitch + row, owner * rows + row] = 1.0
    return tables[0], tables[1], spread, np.ascontiguousarray(spread.T)


def mul(first, second):
    return jnp.dot(first, second, preferred_element_type=jnp.float32)


def mul_t(first, second):
    return lax.dot_general(first, second, (((1,), (1,)), ((), ())), preferred_element_type=jnp.float32)


def sandwich(spread, outer, inner):
    outer_real, outer_imag = outer[0], outer[1]
    inner_real, inner_imag = inner[0], inner[1]
    wide_real = mul(spread, outer_real).astype(jnp.bfloat16)
    wide_imag = mul(spread, outer_imag).astype(jnp.bfloat16)
    half_real = (mul(wide_real, inner_real) - mul(wide_imag, inner_imag)).astype(jnp.bfloat16)
    half_imag = (mul(wide_real, inner_imag) + mul(wide_imag, inner_real)).astype(jnp.bfloat16)
    minus = -outer_imag
    with_real = jnp.concatenate([outer_real[:LANES], minus[:LANES], outer_real[LANES:], minus[LANES:]], axis=0)
    with_imag = jnp.concatenate([outer_imag[:LANES], outer_real[:LANES], outer_imag[LANES:], outer_real[LANES:]], axis=0)
    return mul_t(half_real, with_real) + mul_t(half_imag, with_imag)


def kernel(
    n, slabs, rows, pitch,
    green, couple, sigma, screened, forward, backward, spread, gather,
    out,
    green_v, couple_v, sigma_v, ahead_v, screened_v, forward_v, backward_v, spread_v, gather_v,
    weights, term, send1, recv1, send2, recv2,
    local_sem, slab_send, slab_recv, send1_sem, recv1_sem, send2_sem, recv2_sem,
):
    me = lax.axis_index("energy")
    block = lax.axis_index("slab")
    orbitals = green_v.shape[1]
    length = screened_v.shape[1]
    freq_rows = rows * length
    flat_rows = n * pitch
    tail = orbitals - LANES

    barrier = pltpu.get_barrier_semaphore()

    def greet(step, _):
        pl.semaphore_signal(barrier, inc=1, device_id=(lax.rem(me + step, n), block), device_id_type=MESH)
        return 0

    @pl.when(block > 0)
    def _():
        pl.semaphore_signal(barrier, inc=1, device_id=(me, block - 1), device_id_type=MESH)

    @pl.when(block < slabs - 1)
    def _():
        pl.semaphore_signal(barrier, inc=1, device_id=(me, block + 1), device_id_type=MESH)

    lax.fori_loop(1, n, greet, 0)

    pairs = (
        (green.at[0, 0], green_v), (sigma.at[0, 0], sigma_v), (spread, spread_v), (couple.at[0, 0], couple_v),
        (screened.at[0], screened_v), (forward, forward_v), (backward, backward_v), (gather, gather_v),
    )
    loads = [pltpu.make_async_copy(src, dst, local_sem.at[i]) for i, (src, dst) in enumerate(pairs)]
    for load in loads:
        load.start()

    pl.semaphore_wait(barrier, n - 1 + (block > 0).astype(jnp.int32) + (block < slabs - 1).astype(jnp.int32))

    def to_block_before():
        return pltpu.make_async_remote_copy(
            src_ref=sigma.at[0, 0], dst_ref=ahead_v, send_sem=slab_send, recv_sem=slab_recv,
            device_id=(me, lax.max(block - 1, 0)), device_id_type=MESH,
        )

    @pl.when(block > 0)
    def _():
        to_block_before().start()

    for load in loads[:3]:
        load.wait()
    own = sandwich(spread_v[...], green_v, sigma_v)
    loads[3].wait()

    @pl.when(block == slabs - 1)
    def _():
        send1[...] = own.astype(jnp.bfloat16)

    @pl.when(block < slabs - 1)
    def _():
        term[...] = own
        to_block_before().wait_recv()
        send1[...] = (term[...] + sandwich(spread_v[...], couple_v, ahead_v)).astype(jnp.bfloat16)

    def exchange(src, dst, send_sem, recv_sem):
        def at(ref, index):
            return ref.at[pl.ds(pl.multiple_of(index * pitch, pitch), pitch)]

        def copy(peer, slot):
            return pltpu.make_async_remote_copy(
                src_ref=at(src, peer), dst_ref=at(dst, slot), send_sem=send_sem.at[peer], recv_sem=recv_sem.at[slot],
                device_id=(peer, block), device_id_type=MESH,
            )

        def start(step, _):
            copy(lax.rem(me + step, n), me).start()
            return 0

        def wait_recv(step, _):
            peer = lax.rem(me + step, n)
            copy(peer, peer).wait_recv()
            return 0

        def wait_send(step, _):
            copy(lax.rem(me + step, n), me).wait_send()
            return 0

        lax.fori_loop(1, n, start, 0)
        mine = pl.ds(pl.multiple_of(me * pitch, pitch), pitch)
        dst[mine, :] = src[mine, :]
        return (lambda: lax.fori_loop(1, n, wait_recv, 0)), (lambda: lax.fori_loop(1, n, wait_send, 0))

    arrive1, leave1 = exchange(send1, recv1, send1_sem, recv1_sem)

    loads[4].wait()
    for row in range(rows):
        at = row * orbitals
        where = pl.ds(row * length, length)
        for part in range(2):
            line = screened_v[part, :, at:at + orbitals].astype(jnp.float32)
            last = line[:, LANES:]
            weights[part, where, :LANES] = line[:, :LANES]
            weights[part, where, LANES:] = jnp.concatenate([last, last], axis=1)
    for load in loads[5:]:
        load.wait()

    arrive1()
    arrived = recv1[...]
    by_high = mul(forward_v[:2 * freq_rows], arrived)
    by_low = mul(forward_v[2 * freq_rows:], arrived)
    both = by_high + by_low
    cosine, sine = both[:freq_rows], both[freq_rows:]
    sign = jnp.where(lax.broadcasted_iota(jnp.int32, (1, LANES), 1) < tail, 1.0, -1.0)

    def turn(value):
        return pltpu.roll(value, tail, 1) * sign

    spec_real = cosine[:, :LANES] + sine[:, LANES:2 * LANES]
    spec_imag = cosine[:, LANES:2 * LANES] - sine[:, :LANES]
    spec_tail = cosine[:, 2 * LANES:] + turn(sine[:, 2 * LANES:])
    weight_real, weight_imag = weights[0], weights[1]
    conv = jnp.concatenate(
        [
            spec_real * weight_real[:, :LANES] - spec_imag * weight_imag[:, :LANES],
            spec_real * weight_imag[:, :LANES] + spec_imag * weight_real[:, :LANES],
            spec_tail * weight_real[:, LANES:] - turn(spec_tail) * weight_imag[:, LANES:],
        ],
        axis=1,
    )
    conv_high = conv.astype(jnp.bfloat16)
    conv_low = (conv - conv_high.astype(jnp.float32)).astype(jnp.bfloat16)
    back = mul(backward_v[:2 * flat_rows], conv_high)
    back = back + mul(backward_v[2 * flat_rows:], conv_high)
    back = back + mul(backward_v[:2 * flat_rows], conv_low)
    cosine, sine = back[:flat_rows], back[flat_rows:]
    send2[:, :LANES] = (cosine[:, :LANES] - sine[:, LANES:2 * LANES]).astype(jnp.bfloat16)
    send2[:, LANES:2 * LANES] = (cosine[:, LANES:2 * LANES] + sine[:, :LANES]).astype(jnp.bfloat16)
    send2[:, 2 * LANES:] = (cosine[:, 2 * LANES:] - turn(sine[:, 2 * LANES:])).astype(jnp.bfloat16)

    arrive2, leave2 = exchange(send2, recv2, send2_sem, recv2_sem)
    leave1()

    @pl.when(block > 0)
    def _():
        to_block_before().wait_send()

    arrive2()
    result = mul(gather_v[...], recv2[...]).astype(jnp.bfloat16)
    out[0, 0, 0, :, :LANES] = result[:, :LANES]
    out[0, 0, 1, :, :LANES] = result[:, LANES:2 * LANES]
    out[0, 0, 0, :, LANES:] = result[:, 2 * LANES:2 * LANES + tail]
    out[0, 0, 1, :, LANES:] = result[:, 2 * LANES + tail:]
    leave2()


def shards(n, slabs, green_block, coupling, sigma_lesser, screened):
    orbitals = green_block.shape[-1]
    length = screened.shape[2]
    rows = screened.shape[3] // orbitals
    pitch = -(-rows // PITCH) * PITCH
    assert green_block.shape[0] == 1 and length == 2 * n and rows * n == orbitals and orbitals == LANES + LANES // 2
    tables = make_tables(n, rows, pitch)
    packed = (n * pitch, 2 * orbitals)
    square = (2, orbitals, orbitals)
    bf16 = jnp.bfloat16
    return pl.pallas_call(
        functools.partial(kernel, n, slabs, rows, pitch),
        out_shape=jax.ShapeDtypeStruct(green_block.shape, bf16),
        in_specs=[pl.BlockSpec(memory_space=pl.ANY)] * 8,
        out_specs=pl.BlockSpec(memory_space=pltpu.VMEM),
        scratch_shapes=[
            pltpu.VMEM(square, bf16),
            pltpu.VMEM(square, bf16),
            pltpu.VMEM(square, bf16),
            pltpu.VMEM(square, bf16),
            pltpu.VMEM(screened.shape[1:], bf16),
            *[pltpu.VMEM(table.shape, bf16) for table in tables],
            pltpu.VMEM((2, rows * length, 2 * LANES), jnp.float32),
            pltpu.VMEM(packed, jnp.float32),
            pltpu.VMEM(packed, bf16),
            pltpu.VMEM(packed, bf16),
            pltpu.VMEM(packed, bf16),
            pltpu.VMEM(packed, bf16),
            pltpu.SemaphoreType.DMA((8,)),
            pltpu.SemaphoreType.DMA,
            pltpu.SemaphoreType.DMA,
            *[pltpu.SemaphoreType.DMA((n,))] * 4,
        ],
        compiler_params=pltpu.CompilerParams(
            collective_id=0, has_side_effects=True, vmem_limit_bytes=56 * 1024 * 1024
        ),
        cost_estimate=pl.CostEstimate(flops=10**9, bytes_accessed=4 * 10**6, transcendentals=0),
        name="self_energy",
    )(green_block, coupling, sigma_lesser, screened, *[jnp.asarray(table) for table in tables])


def solution(mesh):
    placed = (
        P("energy", "slab", None, None, None),
        P("energy", "slab", None, None, None),
        P("energy", "slab", None, None, None),
        P("slab", None, None, "energy"),
    )
    return jax.shard_map(
        functools.partial(shards, mesh.shape["energy"], mesh.shape["slab"]),
        mesh=mesh,
        in_specs=placed,
        out_specs=P("energy", "slab", None, None, None),
        check_vma=False,
    )
```

time: 292 us -> 24.3 us (0.08)
  other arithmetic: 167 us -> 0 us
  local copies, waits for them, and re-layouts: 74.6 us -> 1.62 us
  Pallas kernels: 0 us -> 22.5 us
  matrix products: 15 us -> 0 us
  blocking collectives: 11.8 us -> 0 us
  starting transfers between devices: 11.4 us -> 0 us
  waiting for transfers between devices: 11 us -> 0 us
    unnamed x1 -> x0, other arithmetic: 165 us -> none
    unnamed x5 -> x1, local copies, waits for them, and re-layouts: 53 us -> 1.62 us
    pallas_call x0 -> x1, Pallas kernels: none -> 22.5 us  [shards(): pl.pallas_call(functools.partial(kernel, n, slabs, rows, pitch), out_shap...]
    dot_general x18 -> x0, matrix products: 15 us -> none  [the longest x16 13.9 us: product(): return jnp.einsum(form, first, second, preferred_element_type=jnp.float32)]
    all_to_all x1 -> x0, blocking collectives: 11.8 us -> none  [shards(): lax.all_to_all(joined, 'energy', split_axis=0, concat_axis=2, tiled=True)]
    all_to_all x1 -> x0, waiting for transfers between devices: 10.9 us -> none  [shards(): lax.all_to_all(lesser, 'energy', split_axis=2, concat_axis=0, tiled=True)]
    reshape x3 -> x0, local copies, waits for them, and re-layouts: 10.8 us -> none  [the longest x1 9.69 us: shards(): (own_term + far_term).reshape(energies_here, 2, orbitals * orbitals)]
    all_to_all x2 -> x0, local copies, waits for them, and re-layouts: 10.7 us -> none  [the longest x1 10.7 us: shards(): lax.all_to_all(lesser, 'energy', split_axis=2, concat_axis=0, tiled=True)]
  transfers between devices with their start and end apart: 3 -> 0, of which waited for: 1 -> 0; matrix products, arithmetic and copies ran while one was open for 3% -> 0% of each run, Pallas kernels for 0% -> 0%
where the time goes in v1:
time: 24.3 us; the launch traced here: 24.2 us
  Pallas kernels  22.5 us (93%)
  local copies, waits for them, and re-layouts  1.62 us (7%)
    pallas_call x1, Pallas kernels, shards(): pl.pallas_call(functools.partial(kernel, n, slabs, rows, pitch), out_shap...  22.5 us
    unnamed x1, local copies, waits for them, and re-layouts  1.62 us

profile of v1, /device:TPU:0, one launch (start us, length us, event | category | flops | bytes accessed | tf_op | source)
XLA Modules:
  0.0 24.2 jit_solution(10621937114529656046)
XLA Ops:
  0.0 22.5 %self_energy.1 = bf16[1,1,2,192,192]{4,3,2,1,0:T(8,128)(2,1)} custom-call(bf16[1,1,2,192,192]{4,3,2,1,0:T(8,128)(2,1)} %green.1, bf16[1,1,2,192,192]{4,3,2,1,0:T(8,128)(2,1)} %couple.1, bf16[1,1,2,192,192]{4,3,2,1,0:T(8,128)(2,1)} %sigma.1, bf16[1,2,32,2304]{3,2,1,0:T(8,128)(2,1)} %screened.1, bf16[1536,256]{1,0:T(8,128)(2,1)} %constant.8.clone.forward, ...), custom_call_target="tpu_custom_call" | custom-call | flops 1000000000 | bytes 4000000 | tf_op jit(solution)/shard_map/self_energy/pallas_call | solution.py:233
  22.6 1.6 %copy.10 = bf16[1,1,2,192,192]{4,3,2,1,0:T(8,128)(2,1)} copy(bf16[1,1,2,192,192]{4,3,2,1,0:T(8,128)(2,1)} %self_energy.1) | data formatting | bytes 294912

commit v2 on v1

--- a/solution.py
+++ b/solution.py
@@ -64,10 +64,10 @@
 
 def kernel(
     n, slabs, rows, pitch,
-    green, couple, sigma, screened, forward, backward, spread, gather,
-    out,
-    green_v, couple_v, sigma_v, ahead_v, screened_v, forward_v, backward_v, spread_v, gather_v,
-    weights, term, send1, recv1, send2, recv2,
+    green, couple, sigma, screened, forward, backward, spread,
+    recv2,
+    green_v, couple_v, sigma_v, ahead_v, screened_v, forward_v, backward_v, spread_v,
+    weights, term, send1, recv1, send2,
     local_sem, slab_send, slab_recv, send1_sem, recv1_sem, send2_sem, recv2_sem,
 ):
     me = lax.axis_index("energy")
@@ -96,13 +96,14 @@
 
     pairs = (
         (green.at[0, 0], green_v), (sigma.at[0, 0], sigma_v), (spread, spread_v), (couple.at[0, 0], couple_v),
-        (screened.at[0], screened_v), (forward, forward_v), (backward, backward_v), (gather, gather_v),
+        (screened.at[0], screened_v), (forward, forward_v), (backward, backward_v),
     )
     loads = [pltpu.make_async_copy(src, dst, local_sem.at[i]) for i, (src, dst) in enumerate(pairs)]
     for load in loads:
         load.start()
 
-    pl.semaphore_wait(barrier, n - 1 + (block > 0).astype(jnp.int32) + (block < slabs - 1).astype(jnp.int32))
+    def everyone_is_here():
+        pl.semaphore_wait(barrier, n - 1 + (block > 0).astype(jnp.int32) + (block < slabs - 1).astype(jnp.int32))
 
     def to_block_before():
         return pltpu.make_async_remote_copy(
@@ -112,12 +113,17 @@
 
     @pl.when(block > 0)
     def _():
+        everyone_is_here()
         to_block_before().start()
 
     for load in loads[:3]:
         load.wait()
     own = sandwich(spread_v[...], green_v, sigma_v)
     loads[3].wait()
+
+    @pl.when(block == 0)
+    def _():
+        everyone_is_here()
 
     @pl.when(block == slabs - 1)
     def _():
@@ -144,7 +150,7 @@
             return 0
 
         def wait_recv(step, _):
-            peer = lax.rem(me + step, n)
+            peer = lax.rem(me + n - step, n)
             copy(peer, peer).wait_recv()
             return 0
 
@@ -153,8 +159,9 @@
             return 0
 
         lax.fori_loop(1, n, start, 0)
-        mine = pl.ds(pl.multiple_of(me * pitch, pitch), pitch)
-        dst[mine, :] = src[mine, :]
+        keep = pltpu.make_async_copy(at(src, me), at(dst, me), recv_sem.at[me])
+        keep.start()
+        keep.wait()
         return (lambda: lax.fori_loop(1, n, wait_recv, 0)), (lambda: lax.fori_loop(1, n, wait_send, 0))
 
     arrive1, leave1 = exchange(send1, recv1, send1_sem, recv1_sem)
@@ -212,12 +219,16 @@
         to_block_before().wait_send()
 
     arrive2()
-    result = mul(gather_v[...], recv2[...]).astype(jnp.bfloat16)
+    leave2()
+
+
+def unpack(gather, packed, out):
+    tail = out.shape[-1] - LANES
+    result = mul(gather[...], packed[...]).astype(jnp.bfloat16)
     out[0, 0, 0, :, :LANES] = result[:, :LANES]
     out[0, 0, 1, :, :LANES] = result[:, LANES:2 * LANES]
     out[0, 0, 0, :, LANES:] = result[:, 2 * LANES:2 * LANES + tail]
     out[0, 0, 1, :, LANES:] = result[:, 2 * LANES + tail:]
-    leave2()
 
 
 def shards(n, slabs, green_block, coupling, sigma_lesser, screened):
@@ -226,15 +237,15 @@
     rows = screened.shape[3] // orbitals
     pitch = -(-rows // PITCH) * PITCH
     assert green_block.shape[0] == 1 and length == 2 * n and rows * n == orbitals and orbitals == LANES + LANES // 2
-    tables = make_tables(n, rows, pitch)
+    *tables, gather = make_tables(n, rows, pitch)
     packed = (n * pitch, 2 * orbitals)
     square = (2, orbitals, orbitals)
     bf16 = jnp.bfloat16
-    return pl.pallas_call(
+    returned = pl.pallas_call(
         functools.partial(kernel, n, slabs, rows, pitch),
-        out_shape=jax.ShapeDtypeStruct(green_block.shape, bf16),
-        in_specs=[pl.BlockSpec(memory_space=pl.ANY)] * 8,
-        out_specs=pl.BlockSpec(memory_space=pltpu.VMEM),
+        out_shape=jax.ShapeDtypeStruct(packed, bf16),
+        in_specs=[pl.BlockSpec(memory_space=pl.ANY)] * 7,
+        out_specs=pl.BlockSpec(memory_space=pl.ANY),
         scratch_shapes=[
             pltpu.VMEM(square, bf16),
             pltpu.VMEM(square, bf16),
@@ -247,8 +258,7 @@
             pltpu.VMEM(packed, bf16),
             pltpu.VMEM(packed, bf16),
             pltpu.VMEM(packed, bf16),
-            pltpu.VMEM(packed, bf16),
-            pltpu.SemaphoreType.DMA((8,)),
+            pltpu.SemaphoreType.DMA((7,)),
             pltpu.SemaphoreType.DMA,
             pltpu.SemaphoreType.DMA,
             *[pltpu.SemaphoreType.DMA((n,))] * 4,
@@ -259,6 +269,13 @@
         cost_estimate=pl.CostEstimate(flops=10**9, bytes_accessed=4 * 10**6, transcendentals=0),
         name="self_energy",
     )(green_block, coupling, sigma_lesser, screened, *[jnp.asarray(table) for table in tables])
+    return pl.pallas_call(
+        unpack,
+        out_shape=jax.ShapeDtypeStruct(green_block.shape, bf16),
+        in_specs=[pl.BlockSpec(memory_space=pltpu.VMEM)] * 2,
+        out_specs=pl.BlockSpec(memory_space=pltpu.VMEM),
+        name="unpack",
+    )(jnp.asarray(gather), returned)
 
 
 def solution(mesh):

time: 24.3 us -> 23.8 us (0.979)
  local copies, waits for them, and re-layouts: 1.62 us -> 0 us
  Pallas kernels: 22.5 us -> 23.7 us
    pallas_call x0 -> x1, Pallas kernels: none -> 1.91 us  [shards(): pl.pallas_call(unpack, out_shape=jax.ShapeDtypeStruct(green_block.shape,...]
    unnamed x1 -> x0, local copies, waits for them, and re-layouts: 1.62 us -> none
    pallas_call x1, Pallas kernels: 22.5 us -> 21.7 us  [shards(): pl.pallas_call(functools.partial(kernel, n, slabs, rows, pitch), out_shap...]
where the time goes in v2:
time: 23.8 us; the launch traced here: 23.7 us
  Pallas kernels  23.7 us (100%)
    pallas_call x1, Pallas kernels, shards(): pl.pallas_call(functools.partial(kernel, n, slabs, rows, pitch), out_shap...  21.7 us
    pallas_call x1, Pallas kernels, shards(): pl.pallas_call(unpack, out_shape=jax.ShapeDtypeStruct(green_block.shape,...  1.91 us

profile of v2, /device:TPU:0, one launch (start us, length us, event | category | flops | bytes accessed | tf_op | source)
XLA Modules:
  0.0 23.7 jit_solution(9320495336810469787)
XLA Ops:
  0.0 21.7 %self_energy.1.packed = bf16[256,384]{1,0:T(8,128)(2,1)} custom-call(bf16[1,1,2,192,192]{4,3,2,1,0:T(8,128)(2,1)} %green.1, bf16[1,1,2,192,192]{4,3,2,1,0:T(8,128)(2,1)} %couple.1, bf16[1,1,2,192,192]{4,3,2,1,0:T(8,128)(2,1)} %sigma.1, bf16[1,2,32,2304]{3,2,1,0:T(8,128)(2,1)} %screened.1, bf16[1536,256]{1,0:T(8,128)(2,1)} %constant.8.clone.forward, ...), custom_call_target="tpu_custom_call" | custom-call | flops 1000000000 | bytes 4000000 | tf_op jit(solution)/shard_map/self_energy/pallas_call | solution.py:244
  21.8 1.9 %unpack.1 = bf16[1,1,2,192,192]{4,3,2,1,0:T(8,128)(2,1)} custom-call(bf16[192,256]{1,0:T(8,128)(2,1)} %constant.11.clone.gather, bf16[256,384]{1,0:T(8,128)(2,1)} %self_energy.1.packed), custom_call_target="tpu_custom_call" | custom-call | tf_op jit(solution)/shard_map/unpack/pallas_call | solution.py:272

commit v3 on v2

v3 whole, which is shorter than its diff:
```python
import functools

import jax
import jax.numpy as jnp
import ml_dtypes
import numpy as np
from jax import lax
from jax.experimental import pallas as pl
from jax.experimental.pallas import tpu as pltpu
from jax.sharding import PartitionSpec as P

MESH = pl.DeviceIdType.MESH
LANES = 128
PITCH = 16


def split(table):
    high = table.astype(ml_dtypes.bfloat16)
    low = (table - high.astype(np.float64)).astype(ml_dtypes.bfloat16)
    return high, low


def make_tables(count, rows, pitch):
    length = 2 * count
    phases = np.outer(np.arange(count), np.arange(length)) % length
    angles = phases * (2.0 * np.pi / length)
    same = np.zeros((pitch, rows))
    same[np.arange(rows), np.arange(rows)] = 1.0
    high, low = [], []
    for table in (np.cos(angles), np.sin(angles)):
        wide = np.einsum("dk,sr->dsrk", table / length, same).reshape(count * pitch, rows * length)
        for part, into in zip(split(wide), (high, low)):
            into.append(part)
    gather = np.zeros((count * rows, count * pitch), ml_dtypes.bfloat16)
    for owner in range(count):
        for row in range(rows):
            gather[owner * rows + row, owner * pitch + row] = 1.0
    return np.concatenate(high + low, axis=0), gather


def mul(first, second):
    return jnp.dot(first, second, preferred_element_type=jnp.float32)


def mul_t(first, second):
    return lax.dot_general(first, second, (((1,), (1,)), ((), ())), preferred_element_type=jnp.float32)


def sandwich(outer, inner):
    orbitals = outer.shape[1]
    stacked = outer[...].reshape(2 * orbitals, orbitals)
    by_real = mul(stacked, inner[0])
    by_imag = mul(stacked, inner[1])
    half_real = by_real[:orbitals] - by_imag[orbitals:]
    half_imag = by_imag[:orbitals] + by_real[orbitals:]
    half = jnp.concatenate([half_real.astype(jnp.bfloat16), half_imag.astype(jnp.bfloat16)], axis=0)
    with_real = mul_t(half, jnp.concatenate([outer[0], outer[0, LANES:]], axis=0))
    with_imag = mul_t(half, jnp.concatenate([outer[1], outer[1, LANES:]], axis=0))
    full_real = with_real[:orbitals] + with_imag[orbitals:]
    full_imag = with_real[orbitals:] - with_imag[:orbitals]
    low = lax.broadcasted_iota(jnp.int32, (orbitals, LANES), 1) < orbitals - LANES
    return full_real[:, :LANES], full_imag[:, :LANES], jnp.where(low, full_real[:, LANES:], full_imag[:, LANES:])


def kernel(
    n, slabs, rows, pitch,
    green, couple, sigma, screened, inverse,
    recv2,
    green_v, couple_v, sigma_v, ahead_v, screened_v, inverse_v,
    lines, lags, total, term, send1, recv1, send2,
    local_sem, slab_send, slab_recv, send1_sem, recv1_sem, send2_sem, recv2_sem,
):
    me = lax.axis_index("energy")
    block = lax.axis_index("slab")
    orbitals = green_v.shape[1]
    length = screened_v.shape[1]
    lag_rows = n * pitch
    tail = orbitals - LANES

    barrier = pltpu.get_barrier_semaphore()

    def greet(step, _):
        pl.semaphore_signal(barrier, inc=1, device_id=(lax.rem(me + step, n), block), device_id_type=MESH)
        return 0

    @pl.when(block > 0)
    def _():
        pl.semaphore_signal(barrier, inc=1, device_id=(me, block - 1), device_id_type=MESH)

    @pl.when(block < slabs - 1)
    def _():
        pl.semaphore_signal(barrier, inc=1, device_id=(me, block + 1), device_id_type=MESH)

    lax.fori_loop(1, n, greet, 0)

    pairs = (
        (green.at[0, 0], green_v), (sigma.at[0, 0], sigma_v), (couple.at[0, 0], couple_v),
        (screened.at[0], screened_v), (inverse, inverse_v),
    )
    loads = [pltpu.make_async_copy(src, dst, local_sem.at[i]) for i, (src, dst) in enumerate(pairs)]
    for load in loads:
        load.start()

    def everyone_is_here():
        pl.semaphore_wait(barrier, n - 1 + (block > 0).astype(jnp.int32) + (block < slabs - 1).astype(jnp.int32))

    def to_block_before():
        return pltpu.make_async_remote_copy(
            src_ref=sigma.at[0, 0], dst_ref=ahead_v, send_sem=slab_send, recv_sem=slab_recv,
            device_id=(me, lax.max(block - 1, 0)), device_id_type=MESH,
        )

    @pl.when(block > 0)
    def _():
        everyone_is_here()
        to_block_before().start()

    for load in loads[:2]:
        load.wait()
    for group, value in enumerate(sandwich(green_v, sigma_v)):
        term[:orbitals, group * LANES:(group + 1) * LANES] = value
    term[orbitals:] = jnp.zeros((pitch, 3 * LANES), jnp.float32)
    loads[2].wait()

    @pl.when(block == 0)
    def _():
        everyone_is_here()

    @pl.when(block < slabs - 1)
    def _():
        to_block_before().wait_recv()
        for group, value in enumerate(sandwich(couple_v, ahead_v)):
            term[:orbitals, group * LANES:(group + 1) * LANES] += value

    for owner in range(n):
        send1[owner * pitch:(owner + 1) * pitch] = term[owner * rows:owner * rows + pitch].astype(jnp.bfloat16)

    def at(ref, index):
        return ref.at[pl.ds(pl.multiple_of(index * pitch, pitch), pitch)]

    def copy(src, dst, send_sem, recv_sem, peer, slot):
        return pltpu.make_async_remote_copy(
            src_ref=at(src, peer), dst_ref=at(dst, slot), send_sem=send_sem.at[peer], recv_sem=recv_sem.at[slot],
            device_id=(peer, block), device_id_type=MESH,
        )

    def each(act):
        def body(step, _):
            act(step)
            return 0

        lax.fori_loop(1, n, body, 0)

    first = (send1, recv1, send1_sem, recv1_sem)
    second = (send2, recv2, send2_sem, recv2_sem)

    def behind(step):
        return lax.rem(me + n - step, n)

    def ahead(step):
        return lax.rem(me + step, n)

    each(lambda step: copy(*first, ahead(step), me).start())

    loads[3].wait()
    for row in range(rows):
        where = pl.ds(row * length, length)
        for part in range(2):
            line = screened_v[part, :, row * orbitals:(row + 1) * orbitals].astype(jnp.float32)
            last = line[:, LANES:]
            lines[where, part * LANES:(part + 1) * LANES] = line[:, :LANES].astype(jnp.bfloat16)
            lines[where, (part + 2) * LANES:(part + 3) * LANES] = jnp.concatenate([last, last], axis=1).astype(jnp.bfloat16)
    loads[4].wait()
    waves = mul(inverse_v[:2 * lag_rows], lines[...]) + mul(inverse_v[2 * lag_rows:], lines[...])
    cosine, sine = waves[:lag_rows], waves[lag_rows:]
    for group in range(0, 4, 2):
        real, imag = (slice(part * LANES, (part + 1) * LANES) for part in (group, group + 1))
        shape = (n, pitch, LANES)
        lags[n - 1:, :, real] = (cosine[:, real] - sine[:, imag]).reshape(shape)
        lags[n - 1:, :, imag] = (cosine[:, imag] + sine[:, real]).reshape(shape)
        back_real = (cosine[:, real] + sine[:, imag]).reshape(shape)
        back_imag = (cosine[:, imag] - sine[:, real]).reshape(shape)
        for lag in range(1, n):
            lags[n - 1 - lag, :, real] = back_real[lag]
            lags[n - 1 - lag, :, imag] = back_imag[lag]

    sign = jnp.where(lax.broadcasted_iota(jnp.int32, (pitch, LANES), 1) < tail, -1.0, 1.0)
    parts = tuple(slice(part * LANES, (part + 1) * LANES) for part in range(4))

    def take(source, buffer):
        rows_of = buffer[pl.ds(pl.multiple_of(source * pitch, pitch), pitch), :].astype(jnp.float32)
        real, imag, mixed = rows_of[:, parts[0]], rows_of[:, parts[1]], rows_of[:, parts[2]]
        return source, real, imag, mixed, pltpu.roll(mixed, tail, 1) * sign

    def terms(taken, energy):
        source, real, imag, mixed, turned = taken
        lag = energy - source + n - 1
        by_real, by_imag, both_real, both_imag = (lags[lag, :, part] for part in parts)
        return real * by_real - imag * by_imag, real * by_imag + imag * by_real, mixed * both_real + turned * both_imag

    mine = take(me, send1)
    for energy in range(n):
        for part, value in zip(parts, terms(mine, energy)):
            total[energy, :, part] = value

    def arrived(step, _):
        source = behind(step)
        copy(*first, source, source).wait_recv()
        taken = take(source, recv1)
        for energy in range(n):
            for part, value in zip(parts, terms(taken, energy)):
                total[energy, :, part] += value
        return 0

    lax.fori_loop(1, n - 1, arrived, 0)
    source = behind(n - 1)
    copy(*first, source, source).wait_recv()
    taken = take(source, recv1)

    def finish(energy):
        where = pl.ds(pl.multiple_of(energy * pitch, pitch), pitch)
        for part, value in zip(parts, terms(taken, energy)):
            send2[where, part] = (total[energy, :, part] + value).astype(jnp.bfloat16)

    def depart(step):
        finish(ahead(step))
        copy(*second, ahead(step), me).start()

    each(depart)
    finish(me)
    keep = pltpu.make_async_copy(at(send2, me), at(recv2, me), recv2_sem.at[me])
    keep.start()
    each(lambda step: copy(*first, ahead(step), me).wait_send())

    @pl.when(block > 0)
    def _():
        to_block_before().wait_send()

    each(lambda step: copy(*second, behind(step), behind(step)).wait_recv())
    keep.wait()
    each(lambda step: copy(*second, ahead(step), me).wait_send())


def unpack(gather, packed, out):
    tail = out.shape[-1] - LANES
    result = mul(gather[...], packed[...]).astype(jnp.bfloat16)
    out[0, 0, 0, :, :LANES] = result[:, :LANES]
    out[0, 0, 1, :, :LANES] = result[:, LANES:2 * LANES]
    out[0, 0, 0, :, LANES:] = result[:, 2 * LANES:2 * LANES + tail]
    out[0, 0, 1, :, LANES:] = result[:, 2 * LANES + tail:]


def shards(n, slabs, green_block, coupling, sigma_lesser, screened):
    orbitals = green_block.shape[-1]
    length = screened.shape[2]
    rows = screened.shape[3] // orbitals
    pitch = -(-rows // PITCH) * PITCH
    assert green_block.shape[0] == 1 and length == 2 * n and rows * n == orbitals and orbitals == LANES + LANES // 2
    inverse, gather = make_tables(n, rows, pitch)
    packed = (n * pitch, 2 * orbitals)
    square = (2, orbitals, orbitals)
    bf16 = jnp.bfloat16
    returned = pl.pallas_call(
        functools.partial(kernel, n, slabs, rows, pitch),
        out_shape=jax.ShapeDtypeStruct(packed, bf16),
        in_specs=[pl.BlockSpec(memory_space=pl.ANY)] * 5,
        out_specs=pl.BlockSpec(memory_space=pl.ANY),
        scratch_shapes=[
            pltpu.VMEM(square, bf16),
            pltpu.VMEM(square, bf16),
            pltpu.VMEM(square, bf16),
            pltpu.VMEM(square, bf16),
            pltpu.VMEM(screened.shape[1:], bf16),
            pltpu.VMEM(inverse.shape, bf16),
            pltpu.VMEM((rows * length, 4 * LANES), bf16),
            pltpu.VMEM((2 * n - 1, pitch, 4 * LANES), jnp.float32),
            pltpu.VMEM((n, pitch, 3 * LANES), jnp.float32),
            pltpu.VMEM((orbitals + pitch, 3 * LANES), jnp.float32),
            pltpu.VMEM(packed, bf16),
            pltpu.VMEM(packed, bf16),
            pltpu.VMEM(packed, bf16),
            pltpu.SemaphoreType.DMA((5,)),
            pltpu.SemaphoreType.DMA,
            pltpu.SemaphoreType.DMA,
            *[pltpu.SemaphoreType.DMA((n,))] * 4,
        ],
        compiler_params=pltpu.CompilerParams(
            collective_id=0, has_side_effects=True, vmem_limit_bytes=56 * 1024 * 1024
        ),
        cost_estimate=pl.CostEstimate(flops=10**9, bytes_accessed=4 * 10**6, transcendentals=0),
        name="self_energy",
    )(green_block, coupling, sigma_lesser, screened, jnp.asarray(inverse))
    return pl.pallas_call(
        unpack,
        out_shape=jax.ShapeDtypeStruct(green_block.shape, bf16),
        in_specs=[pl.BlockSpec(memory_space=pltpu.VMEM)] * 2,
        out_specs=pl.BlockSpec(memory_space=pltpu.VMEM),
        name="unpack",
    )(jnp.asarray(gather), returned)


def solution(mesh):
    placed = (
        P("energy", "slab", None, None, None),
        P("energy", "slab", None, None, None),
        P("energy", "slab", None, None, None),
        P("slab", None, None, "energy"),
    )
    return jax.shard_map(
        functools.partial(shards, mesh.shape["energy"], mesh.shape["slab"]),
        mesh=mesh,
        in_specs=placed,
        out_specs=P("energy", "slab", None, None, None),
        check_vma=False,
    )
```

time: 23.8 us -> 22.6 us (0.950)
  Pallas kernels: 23.7 us -> 22.5 us
    pallas_call x1, Pallas kernels: 21.7 us -> 20.5 us  [shards(): pl.pallas_call(functools.partial(kernel, n, slabs, rows, pitch), out_shap...]
where the time goes in v3:
time: 22.6 us; the launch traced here: 22.5 us
  Pallas kernels  22.5 us (100%)
    pallas_call x1, Pallas kernels, shards(): pl.pallas_call(functools.partial(kernel, n, slabs, rows, pitch), out_shap...  20.5 us
    pallas_call x1, Pallas kernels, shards(): pl.pallas_call(unpack, out_shape=jax.ShapeDtypeStruct(green_block.shape,...  1.91 us

profile of v3, /device:TPU:0, one launch (start us, length us, event | category | flops | bytes accessed | tf_op | source)
XLA Modules:
  0.0 22.5 jit_solution(894775453655610240)
XLA Ops:
  0.0 20.5 %self_energy.1.packed = bf16[256,384]{1,0:T(8,128)(2,1)} custom-call(bf16[1,1,2,192,192]{4,3,2,1,0:T(8,128)(2,1)} %green.1, bf16[1,1,2,192,192]{4,3,2,1,0:T(8,128)(2,1)} %couple.1, bf16[1,1,2,192,192]{4,3,2,1,0:T(8,128)(2,1)} %sigma.1, bf16[1,2,32,2304]{3,2,1,0:T(8,128)(2,1)} %screened.1, bf16[1024,384]{1,0:T(8,128)(2,1)} %constant.4.clone.inverse), custom_call_target="tpu_custom_call" | custom-call | flops 1000000000 | bytes 4000000 | tf_op jit(solution)/shard_map/self_energy/pallas_call | solution.py:263
  20.6 1.9 %unpack.1 = bf16[1,1,2,192,192]{4,3,2,1,0:T(8,128)(2,1)} custom-call(bf16[192,256]{1,0:T(8,128)(2,1)} %constant.5.clone.gather, bf16[256,384]{1,0:T(8,128)(2,1)} %self_energy.1.packed), custom_call_target="tpu_custom_call" | custom-call | tf_op jit(solution)/shard_map/unpack/pallas_call | solution.py:293

commit v4 on v3

--- a/solution.py
+++ b/solution.py
@@ -46,10 +46,12 @@
     return lax.dot_general(first, second, (((1,), (1,)), ((), ())), preferred_element_type=jnp.float32)
 
 
-def sandwich(outer, inner):
+def sandwich(outer, inner, ready=lambda part: None):
     orbitals = outer.shape[1]
     stacked = outer[...].reshape(2 * orbitals, orbitals)
+    ready(0)
     by_real = mul(stacked, inner[0])
+    ready(1)
     by_imag = mul(stacked, inner[1])
     half_real = by_real[:orbitals] - by_imag[orbitals:]
     half_imag = by_imag[:orbitals] + by_real[orbitals:]
@@ -68,7 +70,7 @@
     recv2,
     green_v, couple_v, sigma_v, ahead_v, screened_v, inverse_v,
     lines, lags, total, term, send1, recv1, send2,
-    local_sem, slab_send, slab_recv, send1_sem, recv1_sem, send2_sem, recv2_sem,
+    local_sem, slab_send, slab_recv, paired, send1_sem, recv1_sem, send2_sem, recv2_sem,
 ):
     me = lax.axis_index("energy")
     block = lax.axis_index("slab")
@@ -79,19 +81,30 @@
 
     barrier = pltpu.get_barrier_semaphore()
 
-    def greet(step, _):
-        pl.semaphore_signal(barrier, inc=1, device_id=(lax.rem(me + step, n), block), device_id_type=MESH)
-        return 0
-
-    @pl.when(block > 0)
-    def _():
-        pl.semaphore_signal(barrier, inc=1, device_id=(me, block - 1), device_id_type=MESH)
-
-    @pl.when(block < slabs - 1)
-    def _():
-        pl.semaphore_signal(barrier, inc=1, device_id=(me, block + 1), device_id_type=MESH)
-
-    lax.fori_loop(1, n, greet, 0)
+    def signal(energy, slab, semaphore=barrier):
+        pl.semaphore_signal(semaphore, inc=1, device_id=(energy, slab), device_id_type=MESH)
+
+    def greet_group():
+        def body(step, _):
+            signal(lax.rem(me + step, n), block)
+            return 0
+
+        lax.fori_loop(1, n, body, 0)
+
+    if slabs == 2:
+        @pl.when(block == 0)
+        def _():
+            signal(me, 1)
+    else:
+        @pl.when(block > 0)
+        def _():
+            signal(me, block - 1)
+
+        @pl.when(block < slabs - 1)
+        def _():
+            signal(me, block + 1)
+
+        greet_group()
 
     pairs = (
         (green.at[0, 0], green_v), (sigma.at[0, 0], sigma_v), (couple.at[0, 0], couple_v),
@@ -101,35 +114,66 @@
     for load in loads:
         load.start()
 
-    def everyone_is_here():
+    half = orbitals // 2
+
+    def to_block_before(part):
+        copies = []
+        for piece in range(2):
+            where = pl.ds(piece * half, half)
+            copies.append(pltpu.make_async_remote_copy(
+                src_ref=sigma_v.at[part, where], dst_ref=ahead_v.at[part, where],
+                send_sem=slab_send.at[2 * part + piece], recv_sem=slab_recv.at[2 * part + piece],
+                device_id=(me, lax.max(block - 1, 0)), device_id_type=MESH,
+            ))
+        return copies
+
+    def send_sigma():
+        for part in range(2):
+            for piece in to_block_before(part):
+                piece.start()
+
+    loads[0].wait()
+    loads[1].wait()
+    if slabs == 2:
+        @pl.when(block == 1)
+        def _():
+            pl.semaphore_wait(barrier, 1)
+            signal(me, 0, paired)
+            send_sigma()
+
+        @pl.when(block == 0)
+        def _():
+            pl.semaphore_wait(paired, 1)
+            greet_group()
+    else:
         pl.semaphore_wait(barrier, n - 1 + (block > 0).astype(jnp.int32) + (block < slabs - 1).astype(jnp.int32))
 
-    def to_block_before():
-        return pltpu.make_async_remote_copy(
-            src_ref=sigma.at[0, 0], dst_ref=ahead_v, send_sem=slab_send, recv_sem=slab_recv,
-            device_id=(me, lax.max(block - 1, 0)), device_id_type=MESH,
-        )
-
-    @pl.when(block > 0)
-    def _():
-        everyone_is_here()
-        to_block_before().start()
-
-    for load in loads[:2]:
-        load.wait()
+        @pl.when(block > 0)
+        def _():
+            send_sigma()
+
     for group, value in enumerate(sandwich(green_v, sigma_v)):
         term[:orbitals, group * LANES:(group + 1) * LANES] = value
     term[orbitals:] = jnp.zeros((pitch, 3 * LANES), jnp.float32)
     loads[2].wait()
 
-    @pl.when(block == 0)
-    def _():
-        everyone_is_here()
+    if slabs == 2:
+        @pl.when(block == 0)
+        def _():
+            pl.semaphore_wait(barrier, n - 1)
+            signal(me, 1)
+
+        @pl.when(block == 1)
+        def _():
+            pl.semaphore_wait(barrier, 1)
+
+    def sigma_is_here(part):
+        for piece in to_block_before(part):
+            piece.wait_recv()
 
     @pl.when(block < slabs - 1)
     def _():
-        to_block_before().wait_recv()
-        for group, value in enumerate(sandwich(couple_v, ahead_v)):
+        for group, value in enumerate(sandwich(couple_v, ahead_v, sigma_is_here)):
             term[:orbitals, group * LANES:(group + 1) * LANES] += value
 
     for owner in range(n):
@@ -234,7 +278,9 @@
 
     @pl.when(block > 0)
     def _():
-        to_block_before().wait_send()
+        for part in range(2):
+            for piece in to_block_before(part):
+                piece.wait_send()
 
     each(lambda step: copy(*second, behind(step), behind(step)).wait_recv())
     keep.wait()
@@ -280,8 +326,9 @@
             pltpu.VMEM(packed, bf16),
             pltpu.VMEM(packed, bf16),
             pltpu.SemaphoreType.DMA((5,)),
-            pltpu.SemaphoreType.DMA,
-            pltpu.SemaphoreType.DMA,
+            pltpu.SemaphoreType.DMA((4,)),
+            pltpu.SemaphoreType.DMA((4,)),
+            pltpu.SemaphoreType.REGULAR,
             *[pltpu.SemaphoreType.DMA((n,))] * 4,
         ],
         compiler_params=pltpu.CompilerParams(

time: 22.6 us -> 23.5 us (1.040)
  Pallas kernels: 22.5 us -> 23.4 us
    pallas_call x1, Pallas kernels: 20.5 us -> 21.5 us  [shards(): pl.pallas_call(functools.partial(kernel, n, slabs, rows, pitch), out_shap...]
where the time goes in v4:
time: 23.5 us; the launch traced here: 23.4 us
  Pallas kernels  23.4 us (100%)
    pallas_call x1, Pallas kernels, shards(): pl.pallas_call(functools.partial(kernel, n, slabs, rows, pitch), out_shap...  21.5 us
    pallas_call x1, Pallas kernels, shards(): pl.pallas_call(unpack, out_shape=jax.ShapeDtypeStruct(green_block.shape,...  1.91 us

profile of v4, /device:TPU:0, one launch (start us, length us, event | category | flops | bytes accessed | tf_op | source)
XLA Modules:
  0.0 23.4 jit_solution(6253789523859846156)
XLA Ops:
  0.0 21.5 %self_energy.1.packed = bf16[256,384]{1,0:T(8,128)(2,1)} custom-call(bf16[1,1,2,192,192]{4,3,2,1,0:T(8,128)(2,1)} %green.1, bf16[1,1,2,192,192]{4,3,2,1,0:T(8,128)(2,1)} %couple.1, bf16[1,1,2,192,192]{4,3,2,1,0:T(8,128)(2,1)} %sigma.1, bf16[1,2,32,2304]{3,2,1,0:T(8,128)(2,1)} %screened.1, bf16[1024,384]{1,0:T(8,128)(2,1)} %constant.4.clone.inverse), custom_call_target="tpu_custom_call" | custom-call | flops 1000000000 | bytes 4000000 | tf_op jit(solution)/shard_map/self_energy/pallas_call | solution.py:309
  21.5 1.9 %unpack.1 = bf16[1,1,2,192,192]{4,3,2,1,0:T(8,128)(2,1)} custom-call(bf16[192,256]{1,0:T(8,128)(2,1)} %constant.5.clone.gather, bf16[256,384]{1,0:T(8,128)(2,1)} %self_energy.1.packed), custom_call_target="tpu_custom_call" | custom-call | tf_op jit(solution)/shard_map/unpack/pallas_call | solution.py:340

commit v5 on v3

--- a/solution.py
+++ b/solution.py
@@ -66,71 +66,80 @@
     n, slabs, rows, pitch,
     green, couple, sigma, screened, inverse,
     recv2,
-    green_v, couple_v, sigma_v, ahead_v, screened_v, inverse_v,
+    outer_v, inner_v, screened_v, inverse_v,
     lines, lags, total, term, send1, recv1, send2,
     local_sem, slab_send, slab_recv, send1_sem, recv1_sem, send2_sem, recv2_sem,
 ):
     me = lax.axis_index("energy")
     block = lax.axis_index("slab")
-    orbitals = green_v.shape[1]
+    orbitals = outer_v.shape[2]
     length = screened_v.shape[1]
     lag_rows = n * pitch
     tail = orbitals - LANES
 
-    barrier = pltpu.get_barrier_semaphore()
-
-    def greet(step, _):
-        pl.semaphore_signal(barrier, inc=1, device_id=(lax.rem(me + step, n), block), device_id_type=MESH)
-        return 0
-
-    @pl.when(block > 0)
-    def _():
-        pl.semaphore_signal(barrier, inc=1, device_id=(me, block - 1), device_id_type=MESH)
-
-    @pl.when(block < slabs - 1)
-    def _():
-        pl.semaphore_signal(barrier, inc=1, device_id=(me, block + 1), device_id_type=MESH)
-
-    lax.fori_loop(1, n, greet, 0)
-
     pairs = (
-        (green.at[0, 0], green_v), (sigma.at[0, 0], sigma_v), (couple.at[0, 0], couple_v),
+        (green.at[0, 0], outer_v.at[0]), (sigma.at[0, 0], inner_v.at[0]), (couple.at[0, 0], outer_v.at[1]),
         (screened.at[0], screened_v), (inverse, inverse_v),
     )
     loads = [pltpu.make_async_copy(src, dst, local_sem.at[i]) for i, (src, dst) in enumerate(pairs)]
-    for load in loads:
+    for load in loads[:2]:
         load.start()
+
+    barrier = pltpu.get_barrier_semaphore()
+
+    def greet(step, _):
+        pl.semaphore_signal(barrier, inc=1, device_id=(lax.rem(me + step, n), block), device_id_type=MESH)
+        return 0
+
+    @pl.when(block > 0)
+    def _():
+        pl.semaphore_signal(barrier, inc=1, device_id=(me, block - 1), device_id_type=MESH)
+
+    @pl.when(block < slabs - 1)
+    def _():
+        pl.semaphore_signal(barrier, inc=1, device_id=(me, block + 1), device_id_type=MESH)
+
+    lax.fori_loop(1, n, greet, 0)
 
     def everyone_is_here():
         pl.semaphore_wait(barrier, n - 1 + (block > 0).astype(jnp.int32) + (block < slabs - 1).astype(jnp.int32))
 
     def to_block_before():
         return pltpu.make_async_remote_copy(
-            src_ref=sigma.at[0, 0], dst_ref=ahead_v, send_sem=slab_send, recv_sem=slab_recv,
+            src_ref=sigma.at[0, 0], dst_ref=inner_v.at[1], send_sem=slab_send, recv_sem=slab_recv,
             device_id=(me, lax.max(block - 1, 0)), device_id_type=MESH,
         )
 
+    term[...] = jnp.zeros_like(term)
+    loads[0].wait()
+    loads[1].wait()
+    for load in loads[2:]:
+        load.start()
+
     @pl.when(block > 0)
     def _():
         everyone_is_here()
         to_block_before().start()
 
-    for load in loads[:2]:
-        load.wait()
-    for group, value in enumerate(sandwich(green_v, sigma_v)):
-        term[:orbitals, group * LANES:(group + 1) * LANES] = value
-    term[orbitals:] = jnp.zeros((pitch, 3 * LANES), jnp.float32)
-    loads[2].wait()
+    def add_term(index, _):
+        @pl.when(index == 1)
+        def _():
+            loads[2].wait()
+            to_block_before().wait_recv()
+
+        for group, value in enumerate(sandwich(outer_v.at[index], inner_v.at[index])):
+            term[:orbitals, group * LANES:(group + 1) * LANES] += value
+        return 0
+
+    lax.fori_loop(0, 1 + (block < slabs - 1).astype(jnp.int32), add_term, 0)
+
+    @pl.when(block == slabs - 1)
+    def _():
+        loads[2].wait()
 
     @pl.when(block == 0)
     def _():
         everyone_is_here()
-
-    @pl.when(block < slabs - 1)
-    def _():
-        to_block_before().wait_recv()
-        for group, value in enumerate(sandwich(couple_v, ahead_v)):
-            term[:orbitals, group * LANES:(group + 1) * LANES] += value
 
     for owner in range(n):
         send1[owner * pitch:(owner + 1) * pitch] = term[owner * rows:owner * rows + pitch].astype(jnp.bfloat16)
@@ -161,6 +170,8 @@
         return lax.rem(me + step, n)
 
     each(lambda step: copy(*first, ahead(step), me).start())
+    own = pltpu.make_async_copy(at(send1, me), at(recv1, me), recv1_sem.at[me])
+    own.start()
 
     loads[3].wait()
     for row in range(rows):
@@ -171,18 +182,28 @@
             lines[where, part * LANES:(part + 1) * LANES] = line[:, :LANES].astype(jnp.bfloat16)
             lines[where, (part + 2) * LANES:(part + 3) * LANES] = jnp.concatenate([last, last], axis=1).astype(jnp.bfloat16)
     loads[4].wait()
-    waves = mul(inverse_v[:2 * lag_rows], lines[...]) + mul(inverse_v[2 * lag_rows:], lines[...])
-    cosine, sine = waves[:lag_rows], waves[lag_rows:]
-    for group in range(0, 4, 2):
-        real, imag = (slice(part * LANES, (part + 1) * LANES) for part in (group, group + 1))
-        shape = (n, pitch, LANES)
-        lags[n - 1:, :, real] = (cosine[:, real] - sine[:, imag]).reshape(shape)
-        lags[n - 1:, :, imag] = (cosine[:, imag] + sine[:, real]).reshape(shape)
-        back_real = (cosine[:, real] + sine[:, imag]).reshape(shape)
-        back_imag = (cosine[:, imag] - sine[:, real]).reshape(shape)
-        for lag in range(1, n):
-            lags[n - 1 - lag, :, real] = back_real[lag]
-            lags[n - 1 - lag, :, imag] = back_imag[lag]
+    count = min(n, 8)
+
+    def make_lags(chunk, _):
+        def waves(kind):
+            high = pl.ds(pl.multiple_of(kind * lag_rows + chunk * count * pitch, count * pitch), count * pitch)
+            low = pl.ds(pl.multiple_of((kind + 2) * lag_rows + chunk * count * pitch, count * pitch), count * pitch)
+            return mul(inverse_v[high], lines[...]) + mul(inverse_v[low], lines[...])
+
+        cosine, sine = waves(0), waves(1)
+        for group in range(0, 4, 2):
+            real, imag = (slice(part * LANES, (part + 1) * LANES) for part in (group, group + 1))
+            for lag in range(count):
+                own = slice(lag * pitch, (lag + 1) * pitch)
+                up = n - 1 + chunk * count + lag
+                down = n - 1 - chunk * count - lag
+                lags[down, :, real] = cosine[own, real] + sine[own, imag]
+                lags[down, :, imag] = cosine[own, imag] - sine[own, real]
+                lags[up, :, real] = cosine[own, real] - sine[own, imag]
+                lags[up, :, imag] = cosine[own, imag] + sine[own, real]
+        return 0
+
+    lax.fori_loop(0, n // count, make_lags, 0)
 
     sign = jnp.where(lax.broadcasted_iota(jnp.int32, (pitch, LANES), 1) < tail, -1.0, 1.0)
     parts = tuple(slice(part * LANES, (part + 1) * LANES) for part in range(4))
@@ -198,21 +219,27 @@
         by_real, by_imag, both_real, both_imag = (lags[lag, :, part] for part in parts)
         return real * by_real - imag * by_imag, real * by_imag + imag * by_real, mixed * both_real + turned * both_imag
 
-    mine = take(me, send1)
-    for energy in range(n):
-        for part, value in zip(parts, terms(mine, energy)):
-            total[energy, :, part] = value
+    def clear(energy, _):
+        total[energy] = jnp.zeros((pitch, 3 * LANES), jnp.float32)
+        return 0
+
+    lax.fori_loop(0, n, clear, 0)
+    own.wait()
 
     def arrived(step, _):
         source = behind(step)
-        copy(*first, source, source).wait_recv()
+
+        @pl.when(step > 0)
+        def _():
+            copy(*first, source, source).wait_recv()
+
         taken = take(source, recv1)
         for energy in range(n):
             for part, value in zip(parts, terms(taken, energy)):
                 total[energy, :, part] += value
         return 0
 
-    lax.fori_loop(1, n - 1, arrived, 0)
+    lax.fori_loop(0, n - 1, arrived, 0)
     source = behind(n - 1)
     copy(*first, source, source).wait_recv()
     taken = take(source, recv1)
@@ -266,10 +293,8 @@
         in_specs=[pl.BlockSpec(memory_space=pl.ANY)] * 5,
         out_specs=pl.BlockSpec(memory_space=pl.ANY),
         scratch_shapes=[
-            pltpu.VMEM(square, bf16),
-            pltpu.VMEM(square, bf16),
-            pltpu.VMEM(square, bf16),
-            pltpu.VMEM(square, bf16),
+            pltpu.VMEM((2, *square), bf16),
+            pltpu.VMEM((2, *square), bf16),
             pltpu.VMEM(screened.shape[1:], bf16),
             pltpu.VMEM(inverse.shape, bf16),
             pltpu.VMEM((rows * length, 4 * LANES), bf16),

time: 22.6 us -> 22.6 us (level)
  no operation moved by 1% of the time
where the time goes in v5:
time: 22.6 us; the launch traced here: 22.4 us
  Pallas kernels  22.4 us (99%)
    pallas_call x1, Pallas kernels, shards(): pl.pallas_call(functools.partial(kernel, n, slabs, rows, pitch), out_shap...  20.5 us
    pallas_call x1, Pallas kernels, shards(): pl.pallas_call(unpack, out_shape=jax.ShapeDtypeStruct(green_block.shape,...  1.91 us

profile of v5, /device:TPU:0, one launch (start us, length us, event | category | flops | bytes accessed | tf_op | source)
XLA Modules:
  0.0 22.4 jit_solution(7205002546803936632)
XLA Ops:
  0.0 20.5 %self_energy.1.packed = bf16[256,384]{1,0:T(8,128)(2,1)} custom-call(bf16[1,1,2,192,192]{4,3,2,1,0:T(8,128)(2,1)} %green.1, bf16[1,1,2,192,192]{4,3,2,1,0:T(8,128)(2,1)} %couple.1, bf16[1,1,2,192,192]{4,3,2,1,0:T(8,128)(2,1)} %sigma.1, bf16[1,2,32,2304]{3,2,1,0:T(8,128)(2,1)} %screened.1, bf16[1024,384]{1,0:T(8,128)(2,1)} %constant.4.clone.inverse), custom_call_target="tpu_custom_call" | custom-call | flops 1000000000 | bytes 4000000 | tf_op jit(solution)/shard_map/self_energy/pallas_call | solution.py:290
  20.5 1.9 %unpack.1 = bf16[1,1,2,192,192]{4,3,2,1,0:T(8,128)(2,1)} custom-call(bf16[192,256]{1,0:T(8,128)(2,1)} %constant.5.clone.gather, bf16[256,384]{1,0:T(8,128)(2,1)} %self_energy.1.packed), custom_call_target="tpu_custom_call" | custom-call | tf_op jit(solution)/shard_map/unpack/pallas_call | solution.py:318

commit v6 on v5

--- a/solution.py
+++ b/solution.py
@@ -66,7 +66,7 @@
     n, slabs, rows, pitch,
     green, couple, sigma, screened, inverse,
     recv2,
-    outer_v, inner_v, screened_v, inverse_v,
+    outer_v, inner_v, sigma_out, sigma_in, screened_v, inverse_v,
     lines, lags, total, term, send1, recv1, send2,
     local_sem, slab_send, slab_recv, send1_sem, recv1_sem, send2_sem, recv2_sem,
 ):
@@ -106,7 +106,7 @@
 
     def to_block_before():
         return pltpu.make_async_remote_copy(
-            src_ref=sigma.at[0, 0], dst_ref=inner_v.at[1], send_sem=slab_send, recv_sem=slab_recv,
+            src_ref=sigma_out, dst_ref=sigma_in, send_sem=slab_send, recv_sem=slab_recv,
             device_id=(me, lax.max(block - 1, 0)), device_id_type=MESH,
         )
 
@@ -118,6 +118,10 @@
 
     @pl.when(block > 0)
     def _():
+        tails = [inner_v[0, part, :, LANES:].astype(jnp.float32) for part in range(2)]
+        sigma_out[:, :LANES] = inner_v[0, 0, :, :LANES]
+        sigma_out[:, LANES:2 * LANES] = inner_v[0, 1, :, :LANES]
+        sigma_out[:, 2 * LANES:] = jnp.concatenate(tails, axis=1).astype(jnp.bfloat16)
         everyone_is_here()
         to_block_before().start()
 
@@ -126,6 +130,11 @@
         def _():
             loads[2].wait()
             to_block_before().wait_recv()
+            inner_v[1, 0, :, :LANES] = sigma_in[:, :LANES]
+            inner_v[1, 1, :, :LANES] = sigma_in[:, LANES:2 * LANES]
+            mixed = sigma_in[:, 2 * LANES:]
+            inner_v[1, 0, :, LANES:] = mixed[:, :tail]
+            inner_v[1, 1, :, LANES:] = mixed[:, tail:]
 
         for group, value in enumerate(sandwich(outer_v.at[index], inner_v.at[index])):
             term[:orbitals, group * LANES:(group + 1) * LANES] += value
@@ -295,6 +304,8 @@
         scratch_shapes=[
             pltpu.VMEM((2, *square), bf16),
             pltpu.VMEM((2, *square), bf16),
+            pltpu.VMEM((orbitals, 3 * LANES), bf16),
+            pltpu.VMEM((orbitals, 3 * LANES), bf16),
             pltpu.VMEM(screened.shape[1:], bf16),
             pltpu.VMEM(inverse.shape, bf16),
             pltpu.VMEM((rows * length, 4 * LANES), bf16),

time: 22.6 us -> 22.8 us (level)
  no operation moved by 1% of the time
where the time goes in v6:
time: 22.8 us; the launch traced here: 22.6 us
  Pallas kernels  22.6 us (99%)
    pallas_call x1, Pallas kernels, shards(): pl.pallas_call(functools.partial(kernel, n, slabs, rows, pitch), out_shap...  20.7 us
    pallas_call x1, Pallas kernels, shards(): pl.pallas_call(unpack, out_shape=jax.ShapeDtypeStruct(green_block.shape,...  1.91 us

profile of v6, /device:TPU:0, one launch (start us, length us, event | category | flops | bytes accessed | tf_op | source)
XLA Modules:
  0.0 22.6 jit_solution(13281362189416854635)
XLA Ops:
  0.0 20.7 %self_energy.1.packed = bf16[256,384]{1,0:T(8,128)(2,1)} custom-call(bf16[1,1,2,192,192]{4,3,2,1,0:T(8,128)(2,1)} %green.1, bf16[1,1,2,192,192]{4,3,2,1,0:T(8,128)(2,1)} %couple.1, bf16[1,1,2,192,192]{4,3,2,1,0:T(8,128)(2,1)} %sigma.1, bf16[1,2,32,2304]{3,2,1,0:T(8,128)(2,1)} %screened.1, bf16[1024,384]{1,0:T(8,128)(2,1)} %constant.4.clone.inverse), custom_call_target="tpu_custom_call" | custom-call | flops 1000000000 | bytes 4000000 | tf_op jit(solution)/shard_map/self_energy/pallas_call | solution.py:299
  20.7 1.9 %unpack.1 = bf16[1,1,2,192,192]{4,3,2,1,0:T(8,128)(2,1)} custom-call(bf16[192,256]{1,0:T(8,128)(2,1)} %constant.5.clone.gather, bf16[256,384]{1,0:T(8,128)(2,1)} %self_energy.1.packed), custom_call_target="tpu_custom_call" | custom-call | tf_op jit(solution)/shard_map/unpack/pallas_call | solution.py:329

commit v7 on v6

--- a/solution.py
+++ b/solution.py
@@ -178,6 +178,10 @@
     def ahead(step):
         return lax.rem(me + step, n)
 
+    @pl.when(block > 0)
+    def _():
+        to_block_before().wait_send()
+
     each(lambda step: copy(*first, ahead(step), me).start())
     own = pltpu.make_async_copy(at(send1, me), at(recv1, me), recv1_sem.at[me])
     own.start()
@@ -267,11 +271,6 @@
     keep = pltpu.make_async_copy(at(send2, me), at(recv2, me), recv2_sem.at[me])
     keep.start()
     each(lambda step: copy(*first, ahead(step), me).wait_send())
-
-    @pl.when(block > 0)
-    def _():
-        to_block_before().wait_send()
-
     each(lambda step: copy(*second, behind(step), behind(step)).wait_recv())
     keep.wait()
     each(lambda step: copy(*second, ahead(step), me).wait_send())
@@ -298,9 +297,9 @@
     bf16 = jnp.bfloat16
     returned = pl.pallas_call(
         functools.partial(kernel, n, slabs, rows, pitch),
-        out_shape=jax.ShapeDtypeStruct(packed, bf16),
+        out_shape=pltpu.VMEM(packed, bf16),
         in_specs=[pl.BlockSpec(memory_space=pl.ANY)] * 5,
-        out_specs=pl.BlockSpec(memory_space=pl.ANY),
+        out_specs=pl.BlockSpec(memory_space=pltpu.VMEM),
         scratch_shapes=[
             pltpu.VMEM((2, *square), bf16),
             pltpu.VMEM((2, *square), bf16),

time: 22.8 us -> 23.3 us (1.022)
  local copies, waits for them, and re-layouts: 0 us -> 0.66 us
    unnamed x0 -> x2, local copies, waits for them, and re-layouts: none -> 0.66 us
where the time goes in v7:
time: 23.3 us; the launch traced here: 23.2 us
  Pallas kernels  22.5 us (97%)
  local copies, waits for them, and re-layouts  0.66 us (3%)
    pallas_call x1, Pallas kernels, shards(): pl.pallas_call(functools.partial(kernel, n, slabs, rows, pitch), out_shap...  20.6 us
    pallas_call x1, Pallas kernels, shards(): pl.pallas_call(unpack, out_shape=jax.ShapeDtypeStruct(green_block.shape,...  1.9 us
    unnamed x2, local copies, waits for them, and re-layouts  0.66 us

profile of v7, /device:TPU:0, one launch (start us, length us, event | category | flops | bytes accessed | tf_op | source)
XLA Modules:
  0.0 23.2 jit_solution(12814186444397871542)
XLA Ops:
  0.0 20.6 %self_energy.1.packed = bf16[256,384]{1,0:T(8,128)(2,1)S(1)} custom-call(bf16[1,1,2,192,192]{4,3,2,1,0:T(8,128)(2,1)} %green.1, bf16[1,1,2,192,192]{4,3,2,1,0:T(8,128)(2,1)} %couple.1, bf16[1,1,2,192,192]{4,3,2,1,0:T(8,128)(2,1)} %sigma.1, bf16[1,2,32,2304]{3,2,1,0:T(8,128)(2,1)} %screened.1, bf16[1024,384]{1,0:T(8,128)(2,1)} %constant.4.clone.inverse), custom_call_target="tpu_custom_call" | custom-call | flops 1000000000 | bytes 4000000 | tf_op jit(solution)/shard_map/self_energy/pallas_call | solution.py:298
  20.6 0.0 copy-start
  20.6 0.7 %copy-done = bf16[256,384]{1,0:T(8,128)(2,1)} copy-done((bf16[256,384]{1,0:T(8,128)(2,1)}, bf16[256,384]{1,0:T(8,128)(2,1)S(1)}, u32[]{:S(2)}) %copy-start) | copy-done | bytes 196632
  21.3 1.9 %unpack.1 = bf16[1,1,2,192,192]{4,3,2,1,0:T(8,128)(2,1)} custom-call(bf16[192,256]{1,0:T(8,128)(2,1)} %constant.5.clone.gather, bf16[256,384]{1,0:T(8,128)(2,1)} %copy-done), custom_call_target="tpu_custom_call" | custom-call | tf_op jit(solution)/shard_map/unpack/pallas_call | solution.py:328
Async XLA Ops:
  20.6 0.7 %copy-start = (bf16[256,384]{1,0:T(8,128)(2,1)}, bf16[256,384]{1,0:T(8,128)(2,1)S(1)}, u32[]{:S(2)}) copy-start(bf16[256,384]{1,0:T(8,128)(2,1)S(1)} %self_energy.1.packed) | copy-start | bytes 589828

commit v8 on v5

--- a/solution.py
+++ b/solution.py
@@ -31,11 +31,7 @@
         wide = np.einsum("dk,sr->dsrk", table / length, same).reshape(count * pitch, rows * length)
         for part, into in zip(split(wide), (high, low)):
             into.append(part)
-    gather = np.zeros((count * rows, count * pitch), ml_dtypes.bfloat16)
-    for owner in range(count):
-        for row in range(rows):
-            gather[owner * rows + row, owner * pitch + row] = 1.0
-    return np.concatenate(high + low, axis=0), gather
+    return np.concatenate(high + low, axis=0)
 
 
 def mul(first, second):
@@ -46,16 +42,15 @@
     return lax.dot_general(first, second, (((1,), (1,)), ((), ())), preferred_element_type=jnp.float32)
 
 
-def sandwich(outer, inner):
-    orbitals = outer.shape[1]
-    stacked = outer[...].reshape(2 * orbitals, orbitals)
+def sandwich(outer, inner, orbitals):
+    stacked = jnp.concatenate([outer[0, :orbitals], outer[1, :orbitals]], axis=0)
     by_real = mul(stacked, inner[0])
     by_imag = mul(stacked, inner[1])
     half_real = by_real[:orbitals] - by_imag[orbitals:]
     half_imag = by_imag[:orbitals] + by_real[orbitals:]
     half = jnp.concatenate([half_real.astype(jnp.bfloat16), half_imag.astype(jnp.bfloat16)], axis=0)
-    with_real = mul_t(half, jnp.concatenate([outer[0], outer[0, LANES:]], axis=0))
-    with_imag = mul_t(half, jnp.concatenate([outer[1], outer[1, LANES:]], axis=0))
+    with_real = mul_t(half, outer[0])
+    with_imag = mul_t(half, outer[1])
     full_real = with_real[:orbitals] + with_imag[orbitals:]
     full_imag = with_real[orbitals:] - with_imag[:orbitals]
     low = lax.broadcasted_iota(jnp.int32, (orbitals, LANES), 1) < orbitals - LANES
@@ -66,19 +61,19 @@
     n, slabs, rows, pitch,
     green, couple, sigma, screened, inverse,
     recv2,
-    outer_v, inner_v, screened_v, inverse_v,
+    green_v, sigma_v, couple_v, sigma_out, sigma_in, outer_v, inner_v, screened_v, inverse_v,
     lines, lags, total, term, send1, recv1, send2,
     local_sem, slab_send, slab_recv, send1_sem, recv1_sem, send2_sem, recv2_sem,
 ):
     me = lax.axis_index("energy")
     block = lax.axis_index("slab")
-    orbitals = outer_v.shape[2]
+    orbitals = green_v.shape[1]
     length = screened_v.shape[1]
     lag_rows = n * pitch
     tail = orbitals - LANES
 
     pairs = (
-        (green.at[0, 0], outer_v.at[0]), (sigma.at[0, 0], inner_v.at[0]), (couple.at[0, 0], outer_v.at[1]),
+        (green.at[0, 0], green_v), (sigma.at[0, 0], sigma_v), (couple.at[0, 0], couple_v),
         (screened.at[0], screened_v), (inverse, inverse_v),
     )
     loads = [pltpu.make_async_copy(src, dst, local_sem.at[i]) for i, (src, dst) in enumerate(pairs)]
@@ -106,11 +101,18 @@
 
     def to_block_before():
         return pltpu.make_async_remote_copy(
-            src_ref=sigma.at[0, 0], dst_ref=inner_v.at[1], send_sem=slab_send, recv_sem=slab_recv,
+            src_ref=sigma_out, dst_ref=sigma_in, send_sem=slab_send, recv_sem=slab_recv,
             device_id=(me, lax.max(block - 1, 0)), device_id_type=MESH,
         )
 
     term[...] = jnp.zeros_like(term)
+    inner_v[...] = jnp.zeros_like(inner_v)
+    outer_v[...] = jnp.zeros_like(outer_v)
+
+    def set_outer(value):
+        outer_v[:, :orbitals, :orbitals] = value[...]
+        outer_v[:, orbitals:, :orbitals] = value[:, LANES:]
+
     loads[0].wait()
     loads[1].wait()
     for load in loads[2:]:
@@ -118,16 +120,29 @@
 
     @pl.when(block > 0)
     def _():
+        tails = [sigma_v[part, :, LANES:].astype(jnp.float32) for part in range(2)]
+        sigma_out[:, :LANES] = sigma_v[0, :, :LANES]
+        sigma_out[:, LANES:2 * LANES] = sigma_v[1, :, :LANES]
+        sigma_out[:, 2 * LANES:] = jnp.concatenate(tails, axis=1).astype(jnp.bfloat16)
         everyone_is_here()
         to_block_before().start()
+
+    set_outer(green_v)
+    inner_v[:, :orbitals, :orbitals] = sigma_v[...]
 
     def add_term(index, _):
         @pl.when(index == 1)
         def _():
             loads[2].wait()
+            set_outer(couple_v)
             to_block_before().wait_recv()
-
-        for group, value in enumerate(sandwich(outer_v.at[index], inner_v.at[index])):
+            inner_v[0, :orbitals, :LANES] = sigma_in[:, :LANES]
+            inner_v[1, :orbitals, :LANES] = sigma_in[:, LANES:2 * LANES]
+            mixed = sigma_in[:, 2 * LANES:]
+            inner_v[0, :orbitals, LANES:orbitals] = mixed[:, :tail]
+            inner_v[1, :orbitals, LANES:orbitals] = mixed[:, tail:]
+
+        for group, value in enumerate(sandwich(outer_v, inner_v, orbitals)):
             term[:orbitals, group * LANES:(group + 1) * LANES] += value
         return 0
 
@@ -268,9 +283,16 @@
     each(lambda step: copy(*second, ahead(step), me).wait_send())
 
 
-def unpack(gather, packed, out):
-    tail = out.shape[-1] - LANES
-    result = mul(gather[...], packed[...]).astype(jnp.bfloat16)
+def unpack(rows, pitch, packed, out):
+    orbitals = out.shape[-1]
+    tail = orbitals - LANES
+    shape = (orbitals, packed.shape[0])
+    to_row = lax.broadcasted_iota(jnp.int32, shape, 0)
+    from_row = lax.broadcasted_iota(jnp.int32, shape, 1)
+    inside = from_row % pitch
+    keep = (inside < rows) & (from_row // pitch * rows + inside == to_row)
+    gather = jnp.where(keep, 1.0, 0.0).astype(jnp.bfloat16)
+    result = mul(gather, packed[...]).astype(jnp.bfloat16)
     out[0, 0, 0, :, :LANES] = result[:, :LANES]
     out[0, 0, 1, :, :LANES] = result[:, LANES:2 * LANES]
     out[0, 0, 0, :, LANES:] = result[:, 2 * LANES:2 * LANES + tail]
@@ -283,18 +305,23 @@
     rows = screened.shape[3] // orbitals
     pitch = -(-rows // PITCH) * PITCH
     assert green_block.shape[0] == 1 and length == 2 * n and rows * n == orbitals and orbitals == LANES + LANES // 2
-    inverse, gather = make_tables(n, rows, pitch)
+    inverse = make_tables(n, rows, pitch)
     packed = (n * pitch, 2 * orbitals)
     square = (2, orbitals, orbitals)
     bf16 = jnp.bfloat16
     returned = pl.pallas_call(
         functools.partial(kernel, n, slabs, rows, pitch),
-        out_shape=jax.ShapeDtypeStruct(packed, bf16),
+        out_shape=pltpu.VMEM(packed, bf16),
         in_specs=[pl.BlockSpec(memory_space=pl.ANY)] * 5,
-        out_specs=pl.BlockSpec(memory_space=pl.ANY),
+        out_specs=pl.BlockSpec(memory_space=pltpu.VMEM),
         scratch_shapes=[
-            pltpu.VMEM((2, *square), bf16),
-            pltpu.VMEM((2, *square), bf16),
+            pltpu.VMEM(square, bf16),
+            pltpu.VMEM(square, bf16),
+            pltpu.VMEM(square, bf16),
+            pltpu.VMEM((orbitals, 3 * LANES), bf16),
+            pltpu.VMEM((orbitals, 3 * LANES), bf16),
+            pltpu.VMEM((2, 2 * LANES, 2 * LANES), bf16),
+            pltpu.VMEM((2, 2 * LANES, 2 * LANES), bf16),
             pltpu.VMEM(screened.shape[1:], bf16),
             pltpu.VMEM(inverse.shape, bf16),
             pltpu.VMEM((rows * length, 4 * LANES), bf16),
@@ -316,12 +343,12 @@
         name="self_energy",
     )(green_block, coupling, sigma_lesser, screened, jnp.asarray(inverse))
     return pl.pallas_call(
-        unpack,
+        functools.partial(unpack, rows, pitch),
         out_shape=jax.ShapeDtypeStruct(green_block.shape, bf16),
-        in_specs=[pl.BlockSpec(memory_space=pltpu.VMEM)] * 2,
+        in_specs=[pl.BlockSpec(memory_space=pltpu.VMEM)],
         out_specs=pl.BlockSpec(memory_space=pltpu.VMEM),
         name="unpack",
-    )(jnp.asarray(gather), returned)
+    )(returned)
 
 
 def solution(mesh):

time: 22.6 us -> 23.4 us (1.035)
  local copies, waits for them, and re-layouts: 0 us -> 0.66 us
    unnamed x0 -> x2, local copies, waits for them, and re-layouts: none -> 0.66 us
where the time goes in v8:
time: 23.4 us; the launch traced here: 23.2 us
  Pallas kernels  22.5 us (96%)
  local copies, waits for them, and re-layouts  0.66 us (3%)
    pallas_call x1, Pallas kernels, shards(): pl.pallas_call(functools.partial(kernel, n, slabs, rows, pitch), out_shap...  20.6 us
    pallas_call x1, Pallas kernels, shards(): pl.pallas_call(functools.partial(unpack, rows, pitch), out_shape=jax.Shap...  1.85 us
    unnamed x2, local copies, waits for them, and re-layouts  0.66 us

profile of v8, /device:TPU:0, one launch (start us, length us, event | category | flops | bytes accessed | tf_op | source)
XLA Modules:
  0.0 23.2 jit_solution(13535513133151344912)
XLA Ops:
  0.0 20.6 %self_energy.1.packed = bf16[256,384]{1,0:T(8,128)(2,1)S(1)} custom-call(bf16[1,1,2,192,192]{4,3,2,1,0:T(8,128)(2,1)} %green.1, bf16[1,1,2,192,192]{4,3,2,1,0:T(8,128)(2,1)} %couple.1, bf16[1,1,2,192,192]{4,3,2,1,0:T(8,128)(2,1)} %sigma.1, bf16[1,2,32,2304]{3,2,1,0:T(8,128)(2,1)} %screened.1, bf16[1024,384]{1,0:T(8,128)(2,1)} %constant.2.clone.inverse), custom_call_target="tpu_custom_call" | custom-call | flops 1000000000 | bytes 4000000 | tf_op jit(solution)/shard_map/self_energy/pallas_call | solution.py:312
  20.7 0.0 copy-start
  20.7 0.7 %copy-done = bf16[256,384]{1,0:T(8,128)(2,1)} copy-done((bf16[256,384]{1,0:T(8,128)(2,1)}, bf16[256,384]{1,0:T(8,128)(2,1)S(1)}, u32[]{:S(2)}) %copy-start) | copy-done | bytes 196632
  21.3 1.9 %unpack.1 = bf16[1,1,2,192,192]{4,3,2,1,0:T(8,128)(2,1)} custom-call(bf16[256,384]{1,0:T(8,128)(2,1)} %copy-done), custom_call_target="tpu_custom_call" | custom-call | tf_op jit(solution)/shard_map/unpack/pallas_call | solution.py:345
Async XLA Ops:
  20.7 0.7 %copy-start = (bf16[256,384]{1,0:T(8,128)(2,1)}, bf16[256,384]{1,0:T(8,128)(2,1)S(1)}, u32[]{:S(2)}) copy-start(bf16[256,384]{1,0:T(8,128)(2,1)S(1)} %self_energy.1.packed) | copy-start | bytes 589828

commit v9 on v5

--- a/solution.py
+++ b/solution.py
@@ -153,12 +153,15 @@
             device_id=(peer, block), device_id_type=MESH,
         )
 
+    def distance(turn):
+        return n // 2 + (turn + 1) // 2 * ((turn + 1) % 2 * 2 - 1)
+
     def each(act):
-        def body(step, _):
-            act(step)
+        def body(turn, _):
+            act(distance(turn))
             return 0
 
-        lax.fori_loop(1, n, body, 0)
+        lax.fori_loop(0, n - 1, body, 0, unroll=n <= 16)
 
     first = (send1, recv1, send1_sem, recv1_sem)
     second = (send2, recv2, send2_sem, recv2_sem)
@@ -219,34 +222,43 @@
         by_real, by_imag, both_real, both_imag = (lags[lag, :, part] for part in parts)
         return real * by_real - imag * by_imag, real * by_imag + imag * by_real, mixed * both_real + turned * both_imag
 
-    def clear(energy, _):
-        total[energy] = jnp.zeros((pitch, 3 * LANES), jnp.float32)
-        return 0
-
-    lax.fori_loop(0, n, clear, 0)
     own.wait()
 
-    def arrived(step, _):
-        source = behind(step)
-
-        @pl.when(step > 0)
-        def _():
+    def both(turn):
+        taken = []
+        for source in (behind(distance(turn)), behind(distance(turn + 1))):
             copy(*first, source, source).wait_recv()
-
-        taken = take(source, recv1)
+            taken.append(take(source, recv1))
+        return taken
+
+    def add(taken, energy):
+        return [one + other for one, other in zip(terms(taken[0], energy), terms(taken[1], energy))]
+
+    mine = take(me, recv1)
+    source = behind(distance(0))
+    copy(*first, source, source).wait_recv()
+    taken = [mine, take(source, recv1)]
+
+    def begin(energy, _):
+        for part, value in zip(parts, add(taken, energy)):
+            total[energy, :, part] = value
+        return 0
+
+    lax.fori_loop(0, n, begin, 0, unroll=n <= 16)
+
+    def arrived(pair, _):
+        taken = both(2 * pair + 1)
         for energy in range(n):
-            for part, value in zip(parts, terms(taken, energy)):
+            for part, value in zip(parts, add(taken, energy)):
                 total[energy, :, part] += value
         return 0
 
-    lax.fori_loop(0, n - 1, arrived, 0)
-    source = behind(n - 1)
-    copy(*first, source, source).wait_recv()
-    taken = take(source, recv1)
+    lax.fori_loop(0, n // 2 - 2, arrived, 0)
+    taken = both(n - 3)
 
     def finish(energy):
         where = pl.ds(pl.multiple_of(energy * pitch, pitch), pitch)
-        for part, value in zip(parts, terms(taken, energy)):
+        for part, value in zip(parts, add(taken, energy)):
             send2[where, part] = (total[energy, :, part] + value).astype(jnp.bfloat16)
 
     def depart(step):
@@ -289,9 +301,9 @@
     bf16 = jnp.bfloat16
     returned = pl.pallas_call(
         functools.partial(kernel, n, slabs, rows, pitch),
-        out_shape=jax.ShapeDtypeStruct(packed, bf16),
+        out_shape=pltpu.VMEM(packed, bf16),
         in_specs=[pl.BlockSpec(memory_space=pl.ANY)] * 5,
-        out_specs=pl.BlockSpec(memory_space=pl.ANY),
+        out_specs=pl.BlockSpec(memory_space=pltpu.VMEM),
         scratch_shapes=[
             pltpu.VMEM((2, *square), bf16),
             pltpu.VMEM((2, *square), bf16),
@@ -321,7 +333,7 @@
         in_specs=[pl.BlockSpec(memory_space=pltpu.VMEM)] * 2,
         out_specs=pl.BlockSpec(memory_space=pltpu.VMEM),
         name="unpack",
-    )(jnp.asarray(gather), returned)
+    )(jnp.asarray(gather), pltpu.with_memory_space_constraint(returned, pltpu.VMEM))
 
 
 def solution(mesh):

time: 22.6 us -> 23.7 us (1.049)
  Pallas kernels: 22.4 us -> 23.6 us
    pallas_call x1, Pallas kernels: 20.5 us -> 21.7 us  [shards(): pl.pallas_call(functools.partial(kernel, n, slabs, rows, pitch), out_shap...]
where the time goes in v9:
time: 23.7 us; the launch traced here: 23.6 us
  Pallas kernels  23.6 us (100%)
    pallas_call x1, Pallas kernels, shards(): pl.pallas_call(functools.partial(kernel, n, slabs, rows, pitch), out_shap...  21.7 us
    pallas_call x1, Pallas kernels, shards(): pl.pallas_call(unpack, out_shape=jax.ShapeDtypeStruct(green_block.shape,...  1.83 us

profile of v9, /device:TPU:0, one launch (start us, length us, event | category | flops | bytes accessed | tf_op | source)
XLA Modules:
  0.0 23.6 jit_solution(18246298146232566886)
XLA Ops:
  0.0 21.7 %self_energy.1.packed = bf16[256,384]{1,0:T(8,128)(2,1)S(1)} custom-call(bf16[1,1,2,192,192]{4,3,2,1,0:T(8,128)(2,1)} %green.1, bf16[1,1,2,192,192]{4,3,2,1,0:T(8,128)(2,1)} %couple.1, bf16[1,1,2,192,192]{4,3,2,1,0:T(8,128)(2,1)} %sigma.1, bf16[1,2,32,2304]{3,2,1,0:T(8,128)(2,1)} %screened.1, bf16[1024,384]{1,0:T(8,128)(2,1)} %constant.4.clone.inverse), custom_call_target="tpu_custom_call" | custom-call | flops 1000000000 | bytes 4000000 | tf_op jit(solution)/shard_map/self_energy/pallas_call | solution.py:302
  21.7 1.8 %unpack.1 = bf16[1,1,2,192,192]{4,3,2,1,0:T(8,128)(2,1)} custom-call(bf16[192,256]{1,0:T(8,128)(2,1)} %constant.5.clone.gather, bf16[256,384]{1,0:T(8,128)(2,1)S(1)} %self_energy.1.packed), custom_call_target="tpu_custom_call" | custom-call | tf_op jit(solution)/shard_map/unpack/pallas_call | solution.py:330

commit v10 on v9

--- a/solution.py
+++ b/solution.py
@@ -31,11 +31,7 @@
         wide = np.einsum("dk,sr->dsrk", table / length, same).reshape(count * pitch, rows * length)
         for part, into in zip(split(wide), (high, low)):
             into.append(part)
-    gather = np.zeros((count * rows, count * pitch), ml_dtypes.bfloat16)
-    for owner in range(count):
-        for row in range(rows):
-            gather[owner * rows + row, owner * pitch + row] = 1.0
-    return np.concatenate(high + low, axis=0), gather
+    return np.concatenate(high + low, axis=0)
 
 
 def mul(first, second):
@@ -154,7 +150,7 @@
         )
 
     def distance(turn):
-        return n // 2 + (turn + 1) // 2 * ((turn + 1) % 2 * 2 - 1)
+        return turn + 1
 
     def each(act):
         def body(turn, _):
@@ -280,9 +276,13 @@
     each(lambda step: copy(*second, ahead(step), me).wait_send())
 
 
-def unpack(gather, packed, out):
-    tail = out.shape[-1] - LANES
-    result = mul(gather[...], packed[...]).astype(jnp.bfloat16)
+def unpack(rows, pitch, packed, out, spread):
+    orbitals = out.shape[-1]
+    tail = orbitals - LANES
+    for owner in range(orbitals // rows):
+        block = packed[owner * pitch:(owner + 1) * pitch].astype(jnp.float32)
+        spread[owner * rows:owner * rows + pitch] = block
+    result = spread[:orbitals].astype(jnp.bfloat16)
     out[0, 0, 0, :, :LANES] = result[:, :LANES]
     out[0, 0, 1, :, :LANES] = result[:, LANES:2 * LANES]
     out[0, 0, 0, :, LANES:] = result[:, 2 * LANES:2 * LANES + tail]
@@ -295,7 +295,7 @@
     rows = screened.shape[3] // orbitals
     pitch = -(-rows // PITCH) * PITCH
     assert green_block.shape[0] == 1 and length == 2 * n and rows * n == orbitals and orbitals == LANES + LANES // 2
-    inverse, gather = make_tables(n, rows, pitch)
+    inverse = make_tables(n, rows, pitch)
     packed = (n * pitch, 2 * orbitals)
     square = (2, orbitals, orbitals)
     bf16 = jnp.bfloat16
@@ -328,12 +328,13 @@
         name="self_energy",
     )(green_block, coupling, sigma_lesser, screened, jnp.asarray(inverse))
     return pl.pallas_call(
-        unpack,
+        functools.partial(unpack, rows, pitch),
         out_shape=jax.ShapeDtypeStruct(green_block.shape, bf16),
-        in_specs=[pl.BlockSpec(memory_space=pltpu.VMEM)] * 2,
+        in_specs=[pl.BlockSpec(memory_space=pltpu.VMEM)],
         out_specs=pl.BlockSpec(memory_space=pltpu.VMEM),
+        scratch_shapes=[pltpu.VMEM((orbitals + pitch, 3 * LANES), jnp.float32)],
         name="unpack",
-    )(jnp.asarray(gather), pltpu.with_memory_space_constraint(returned, pltpu.VMEM))
+    )(pltpu.with_memory_space_constraint(returned, pltpu.VMEM))
 
 
 def solution(mesh):

time: 23.7 us -> 21.2 us (0.89)
  Pallas kernels: 23.6 us -> 21.1 us
    pallas_call x1, Pallas kernels: 21.7 us -> 20.2 us  [shards(): pl.pallas_call(functools.partial(kernel, n, slabs, rows, pitch), out_shap...]
    pallas_call x1, Pallas kernels: 1.83 us -> 0.81 us  [shards(): pl.pallas_call(functools.partial(unpack, rows, pitch), out_shape=jax.Shap...]
where the time goes in v10:
time: 21.2 us; the launch traced here: 21.1 us
  Pallas kernels  21.1 us (100%)
    pallas_call x1, Pallas kernels, shards(): pl.pallas_call(functools.partial(kernel, n, slabs, rows, pitch), out_shap...  20.2 us
    pallas_call x1, Pallas kernels, shards(): pl.pallas_call(functools.partial(unpack, rows, pitch), out_shape=jax.Shap...  0.81 us

profile of v10, /device:TPU:0, one launch (start us, length us, event | category | flops | bytes accessed | tf_op | source)
XLA Modules:
  0.0 21.1 jit_solution(2868109781088412109)
XLA Ops:
  0.0 20.2 %self_energy.1.packed = bf16[256,384]{1,0:T(8,128)(2,1)S(1)} custom-call(bf16[1,1,2,192,192]{4,3,2,1,0:T(8,128)(2,1)} %green.1, bf16[1,1,2,192,192]{4,3,2,1,0:T(8,128)(2,1)} %couple.1, bf16[1,1,2,192,192]{4,3,2,1,0:T(8,128)(2,1)} %sigma.1, bf16[1,2,32,2304]{3,2,1,0:T(8,128)(2,1)} %screened.1, bf16[1024,384]{1,0:T(8,128)(2,1)} %constant.2.clone.inverse), custom_call_target="tpu_custom_call" | custom-call | flops 1000000000 | bytes 4000000 | tf_op jit(solution)/shard_map/self_energy/pallas_call | solution.py:302
  20.3 0.8 %unpack.1 = bf16[1,1,2,192,192]{4,3,2,1,0:T(8,128)(2,1)} custom-call(bf16[256,384]{1,0:T(8,128)(2,1)S(1)} %self_energy.1.packed), custom_call_target="tpu_custom_call" | custom-call | tf_op jit(solution)/shard_map/unpack/pallas_call | solution.py:330

commit v11 on v10

--- a/solution.py
+++ b/solution.py
@@ -45,13 +45,14 @@
 def sandwich(outer, inner):
     orbitals = outer.shape[1]
     stacked = outer[...].reshape(2 * orbitals, orbitals)
-    by_real = mul(stacked, inner[0])
-    by_imag = mul(stacked, inner[1])
+    both = mul(stacked, inner[...])
+    by_real, by_imag = both[:, :orbitals], both[:, 2 * LANES:2 * LANES + orbitals]
     half_real = by_real[:orbitals] - by_imag[orbitals:]
     half_imag = by_imag[:orbitals] + by_real[orbitals:]
     half = jnp.concatenate([half_real.astype(jnp.bfloat16), half_imag.astype(jnp.bfloat16)], axis=0)
-    with_real = mul_t(half, jnp.concatenate([outer[0], outer[0, LANES:]], axis=0))
-    with_imag = mul_t(half, jnp.concatenate([outer[1], outer[1, LANES:]], axis=0))
+    right = jnp.concatenate([outer[0], outer[0, LANES:], outer[1], outer[1, LANES:]], axis=0)
+    both = mul_t(half, right)
+    with_real, with_imag = both[:, :2 * LANES], both[:, 2 * LANES:]
     full_real = with_real[:orbitals] + with_imag[orbitals:]
     full_imag = with_real[orbitals:] - with_imag[:orbitals]
     low = lax.broadcasted_iota(jnp.int32, (orbitals, LANES), 1) < orbitals - LANES
@@ -62,7 +63,7 @@
     n, slabs, rows, pitch,
     green, couple, sigma, screened, inverse,
     recv2,
-    outer_v, inner_v, screened_v, inverse_v,
+    outer_v, sigma_v, inner_v, screened_v, inverse_v,
     lines, lags, total, term, send1, recv1, send2,
     local_sem, slab_send, slab_recv, send1_sem, recv1_sem, send2_sem, recv2_sem,
 ):
@@ -74,7 +75,7 @@
     tail = orbitals - LANES
 
     pairs = (
-        (green.at[0, 0], outer_v.at[0]), (sigma.at[0, 0], inner_v.at[0]), (couple.at[0, 0], outer_v.at[1]),
+        (green.at[0, 0], outer_v.at[0]), (sigma.at[0, 0], sigma_v.at[0]), (couple.at[0, 0], outer_v.at[1]),
         (screened.at[0], screened_v), (inverse, inverse_v),
     )
     loads = [pltpu.make_async_copy(src, dst, local_sem.at[i]) for i, (src, dst) in enumerate(pairs)]
@@ -102,11 +103,12 @@
 
     def to_block_before():
         return pltpu.make_async_remote_copy(
-            src_ref=sigma.at[0, 0], dst_ref=inner_v.at[1], send_sem=slab_send, recv_sem=slab_recv,
+            src_ref=sigma.at[0, 0], dst_ref=sigma_v.at[1], send_sem=slab_send, recv_sem=slab_recv,
             device_id=(me, lax.max(block - 1, 0)), device_id_type=MESH,
         )
 
     term[...] = jnp.zeros_like(term)
+    inner_v[...] = jnp.zeros_like(inner_v)
     loads[0].wait()
     loads[1].wait()
     for load in loads[2:]:
@@ -123,7 +125,9 @@
             loads[2].wait()
             to_block_before().wait_recv()
 
-        for group, value in enumerate(sandwich(outer_v.at[index], inner_v.at[index])):
+        inner_v[:, :orbitals] = sigma_v[index, 0]
+        inner_v[:, 2 * LANES:2 * LANES + orbitals] = sigma_v[index, 1]
+        for group, value in enumerate(sandwich(outer_v.at[index], inner_v)):
             term[:orbitals, group * LANES:(group + 1) * LANES] += value
         return 0
 
@@ -181,28 +185,18 @@
             lines[where, part * LANES:(part + 1) * LANES] = line[:, :LANES].astype(jnp.bfloat16)
             lines[where, (part + 2) * LANES:(part + 3) * LANES] = jnp.concatenate([last, last], axis=1).astype(jnp.bfloat16)
     loads[4].wait()
-    count = min(n, 8)
-
-    def make_lags(chunk, _):
-        def waves(kind):
-            high = pl.ds(pl.multiple_of(kind * lag_rows + chunk * count * pitch, count * pitch), count * pitch)
-            low = pl.ds(pl.multiple_of((kind + 2) * lag_rows + chunk * count * pitch, count * pitch), count * pitch)
-            return mul(inverse_v[high], lines[...]) + mul(inverse_v[low], lines[...])
-
-        cosine, sine = waves(0), waves(1)
-        for group in range(0, 4, 2):
-            real, imag = (slice(part * LANES, (part + 1) * LANES) for part in (group, group + 1))
-            for lag in range(count):
-                own = slice(lag * pitch, (lag + 1) * pitch)
-                up = n - 1 + chunk * count + lag
-                down = n - 1 - chunk * count - lag
-                lags[down, :, real] = cosine[own, real] + sine[own, imag]
-                lags[down, :, imag] = cosine[own, imag] - sine[own, real]
-                lags[up, :, real] = cosine[own, real] - sine[own, imag]
-                lags[up, :, imag] = cosine[own, imag] + sine[own, real]
-        return 0
-
-    lax.fori_loop(0, n // count, make_lags, 0)
+    waves = mul(inverse_v[...], lines[...])
+    cosine = waves[:lag_rows] + waves[2 * lag_rows:3 * lag_rows]
+    sine = waves[lag_rows:2 * lag_rows] + waves[3 * lag_rows:]
+    for group in range(0, 4, 2):
+        real, imag = (slice(part * LANES, (part + 1) * LANES) for part in (group, group + 1))
+        for lag in range(n):
+            here = slice(lag * pitch, (lag + 1) * pitch)
+            lags[n - 1 + lag, :, real] = cosine[here, real] - sine[here, imag]
+            lags[n - 1 + lag, :, imag] = cosine[here, imag] + sine[here, real]
+            if lag > 0:
+                lags[n - 1 - lag, :, real] = cosine[here, real] + sine[here, imag]
+                lags[n - 1 - lag, :, imag] = cosine[here, imag] - sine[here, real]
 
     sign = jnp.where(lax.broadcasted_iota(jnp.int32, (pitch, LANES), 1) < tail, -1.0, 1.0)
     parts = tuple(slice(part * LANES, (part + 1) * LANES) for part in range(4))
@@ -307,6 +301,7 @@
         scratch_shapes=[
             pltpu.VMEM((2, *square), bf16),
             pltpu.VMEM((2, *square), bf16),
+            pltpu.VMEM((orbitals, 4 * LANES), bf16),
             pltpu.VMEM(screened.shape[1:], bf16),
             pltpu.VMEM(inverse.shape, bf16),
             pltpu.VMEM((rows * length, 4 * LANES), bf16),

time: 21.2 us -> 21.2 us (level)
  no operation moved by 1% of the time
where the time goes in v11:
time: 21.2 us; the launch traced here: 21.1 us
  Pallas kernels  21.1 us (100%)
    pallas_call x1, Pallas kernels, shards(): pl.pallas_call(functools.partial(kernel, n, slabs, rows, pitch), out_shap...  20.3 us
    pallas_call x1, Pallas kernels, shards(): pl.pallas_call(functools.partial(unpack, rows, pitch), out_shape=jax.Shap...  0.81 us

profile of v11, /device:TPU:0, one launch (start us, length us, event | category | flops | bytes accessed | tf_op | source)
XLA Modules:
  0.0 21.1 jit_solution(13579522445265367155)
XLA Ops:
  0.0 20.3 %self_energy.1.packed = bf16[256,384]{1,0:T(8,128)(2,1)S(1)} custom-call(bf16[1,1,2,192,192]{4,3,2,1,0:T(8,128)(2,1)} %green.1, bf16[1,1,2,192,192]{4,3,2,1,0:T(8,128)(2,1)} %couple.1, bf16[1,1,2,192,192]{4,3,2,1,0:T(8,128)(2,1)} %sigma.1, bf16[1,2,32,2304]{3,2,1,0:T(8,128)(2,1)} %screened.1, bf16[1024,384]{1,0:T(8,128)(2,1)} %constant.2.clone.inverse), custom_call_target="tpu_custom_call" | custom-call | flops 1000000000 | bytes 4000000 | tf_op jit(solution)/shard_map/self_energy/pallas_call | solution.py:296
  20.3 0.8 %unpack.1 = bf16[1,1,2,192,192]{4,3,2,1,0:T(8,128)(2,1)} custom-call(bf16[256,384]{1,0:T(8,128)(2,1)S(1)} %self_energy.1.packed), custom_call_target="tpu_custom_call" | custom-call | tf_op jit(solution)/shard_map/unpack/pallas_call | solution.py:325

commit v12 on v11

--- a/solution.py
+++ b/solution.py
@@ -14,24 +14,17 @@
 PITCH = 16
 
 
-def split(table):
-    high = table.astype(ml_dtypes.bfloat16)
-    low = (table - high.astype(np.float64)).astype(ml_dtypes.bfloat16)
-    return high, low
-
-
 def make_tables(count, rows, pitch):
     length = 2 * count
     phases = np.outer(np.arange(count), np.arange(length)) % length
     angles = phases * (2.0 * np.pi / length)
     same = np.zeros((pitch, rows))
     same[np.arange(rows), np.arange(rows)] = 1.0
-    high, low = [], []
+    tables = []
     for table in (np.cos(angles), np.sin(angles)):
         wide = np.einsum("dk,sr->dsrk", table / length, same).reshape(count * pitch, rows * length)
-        for part, into in zip(split(wide), (high, low)):
-            into.append(part)
-    return np.concatenate(high + low, axis=0)
+        tables.append(wide.astype(ml_dtypes.bfloat16))
+    return np.concatenate(tables, axis=0)
 
 
 def mul(first, second):
@@ -186,8 +179,7 @@
             lines[where, (part + 2) * LANES:(part + 3) * LANES] = jnp.concatenate([last, last], axis=1).astype(jnp.bfloat16)
     loads[4].wait()
     waves = mul(inverse_v[...], lines[...])
-    cosine = waves[:lag_rows] + waves[2 * lag_rows:3 * lag_rows]
-    sine = waves[lag_rows:2 * lag_rows] + waves[3 * lag_rows:]
+    cosine, sine = waves[:lag_rows], waves[lag_rows:]
     for group in range(0, 4, 2):
         real, imag = (slice(part * LANES, (part + 1) * LANES) for part in (group, group + 1))
         for lag in range(n):

time: 21.2 us -> 21.2 us (level)
  no operation moved by 1% of the time
where the time goes in v12:
time: 21.2 us; the launch traced here: 21.1 us
  Pallas kernels  21.1 us (100%)
    pallas_call x1, Pallas kernels, shards(): pl.pallas_call(functools.partial(kernel, n, slabs, rows, pitch), out_shap...  20.3 us
    pallas_call x1, Pallas kernels, shards(): pl.pallas_call(functools.partial(unpack, rows, pitch), out_shape=jax.Shap...  0.81 us

profile of v12, /device:TPU:0, one launch (start us, length us, event | category | flops | bytes accessed | tf_op | source)
XLA Modules:
  0.0 21.1 jit_solution(16542419273794396909)
XLA Ops:
  0.0 20.3 %self_energy.1.packed = bf16[256,384]{1,0:T(8,128)(2,1)S(1)} custom-call(bf16[1,1,2,192,192]{4,3,2,1,0:T(8,128)(2,1)} %green.1, bf16[1,1,2,192,192]{4,3,2,1,0:T(8,128)(2,1)} %couple.1, bf16[1,1,2,192,192]{4,3,2,1,0:T(8,128)(2,1)} %sigma.1, bf16[1,2,32,2304]{3,2,1,0:T(8,128)(2,1)} %screened.1, bf16[512,384]{1,0:T(8,128)(2,1)} %constant.2.clone.inverse), custom_call_target="tpu_custom_call" | custom-call | flops 1000000000 | bytes 4000000 | tf_op jit(solution)/shard_map/self_energy/pallas_call | solution.py:288
  20.3 0.8 %unpack.1 = bf16[1,1,2,192,192]{4,3,2,1,0:T(8,128)(2,1)} custom-call(bf16[256,384]{1,0:T(8,128)(2,1)S(1)} %self_energy.1.packed), custom_call_target="tpu_custom_call" | custom-call | tf_op jit(solution)/shard_map/unpack/pallas_call | solution.py:317
